TPU v7x, 32 devices: a whole 2x2x4 slice. The times are simulated.
32 devices in a mesh: head: 2 (over y), blk: 16 (over z, x, core).
Axes of the slice: x: 2, y: 2, z: 4, core: 2. Of those that a mesh axis runs over, the one named last changes fastest.
Arguments:
- block_input: bfloat16 [2, 4096, 1024], P(None, ('blk', 'head')), may hold values from -6 to 6
- qkv_weight: bfloat16 [1024, 3072], P(('blk', 'head')), may hold values from -0.1875 to 0.1875
- q_bias: bfloat16 [1024], P(('blk', 'head')), may hold values from -3 to 3
- v_bias: bfloat16 [1024], P(('blk', 'head')), may hold values from -0.3125 to 0.3125
- out_weight: bfloat16 [1024, 1024], P(('blk', 'head')), may hold values from -3 to 3
- out_bias: bfloat16 [1024], P(('blk', 'head')), may hold values from -3 to 3
- norm1_gain: bfloat16 [1024], P(('blk', 'head')), may hold values from 0.099609375 to 1.8984375
- norm1_shift: bfloat16 [1024], P(('blk', 'head')), may hold values from -3 to 3
- norm2_gain: bfloat16 [1024], P(('blk', 'head')), may hold values from 0.099609375 to 1.8984375
- norm2_shift: bfloat16 [1024], P(('blk', 'head')), may hold values from -3 to 3
- fc_weight: bfloat16 [1024, 4096], P(('blk', 'head')), may hold values from -0.1875 to 0.1875
- fc_bias: bfloat16 [4096], P(('blk', 'head')), may hold values from -3 to 3
- proj_weight: bfloat16 [4096, 1024], P(('blk', 'head')), may hold values from -0.09375 to 0.09375
- proj_bias: bfloat16 [1024], P(('blk', 'head')), may hold values from -3 to 3
- out_grad: bfloat16 [2, 4096, 1024], P(None, ('blk', 'head')), may hold values from -6 to 6
- dealt: int32 [2, 4096], replicated, may hold values from 0 to 4095, as said below
- lengths: int32 [2, 2], replicated, may hold values from 1024 to 3072, as said below
Outputs:
- block_output: bfloat16 [2, 4096, 1024], P(None, ('blk', 'head'))
- input_grad: bfloat16 [2, 4096, 1024], P(None, ('blk', 'head'))
- grad_qkv_weight: float32 [1024, 3072], P(('blk', 'head'))
- grad_q_bias: float32 [1024], P(('blk', 'head'))
- grad_v_bias: float32 [1024], P(('blk', 'head'))
- grad_out_weight: float32 [1024, 1024], P(('blk', 'head'))
- grad_out_bias: float32 [1024], P(('blk', 'head'))
- grad_norm1_gain: float32 [1024], P(('blk', 'head'))
- grad_norm1_shift: float32 [1024], P(('blk', 'head'))
- grad_norm2_gain: float32 [1024], P(('blk', 'head'))
- grad_norm2_shift: float32 [1024], P(('blk', 'head'))
- grad_fc_weight: float32 [1024, 4096], P(('blk', 'head'))
- grad_fc_bias: float32 [4096], P(('blk', 'head'))
- grad_proj_weight: float32 [4096, 1024], P(('blk', 'head'))
- grad_proj_bias: float32 [1024], P(('blk', 'head'))
Inputs may be any that keep to these rules, and one draw needn't show every extreme that they name: `dealt`: row b is a permutation of 0 to 4095: entry j is the packed position of the j-th stored token. Cut the packed order into 64 runs of 64 positions; each consecutive group of 128 stored tokens is run t followed by run 2 * 32 - 1 - t, each ascending, for a t of its own. Row b gives the lengths of micro-batch b's two sequences in packed order (the first holds the positions below lengths[b, 0]); they add up to 4096.
All inputs are finite; a program needn't handle non-finite values.
Results may differ from a plain program's by a relative error of at most 0.024.
Values may be sent and summed in bfloat16 or wider, within the bound.
No kernel may reach another device: no remote copies, remote signals or barrier semaphores. Data moves between devices by JAX's collectives and lax.ppermute only.
A program may use at most 384 MiB of HBM per device.

v0:
```python
import math

import jax
import jax.numpy as jnp
from jax import lax
from jax.sharding import PartitionSpec as P

DH = 64


def gelu_tanh(values):
    inner = 0.7978845608028654 * (values + 0.044715 * values * values * values)
    return 0.5 * values * (1.0 + jnp.tanh(inner))


def normalize(values):
    centred = values - jnp.mean(values, axis=-1, keepdims=True)
    inverse = lax.rsqrt(jnp.mean(centred * centred, axis=-1, keepdims=True) + 1e-05)
    return (centred * inverse, inverse)


def norm_back(grad_normed, normed, inverse):
    return inverse * (
        grad_normed
        - jnp.mean(grad_normed, axis=-1, keepdims=True)
        - normed * jnp.mean(grad_normed * normed, axis=-1, keepdims=True)
    )


def product(left, right):
    return jnp.dot(left, right, preferred_element_type=jnp.float32)


def product_tn(left, right):
    return lax.dot_general(
        left, right, (((0,), (0,)), ((), ())), preferred_element_type=jnp.float32
    )


def product_nt(left, right):
    return lax.dot_general(
        left, right, (((1,), (1,)), ((), ())), preferred_element_type=jnp.float32
    )


def visible_pairs(query_pos, key_pos, boundary):
    same_side = (query_pos[:, None] >= boundary) == (key_pos[None, :] >= boundary)
    return same_side & (key_pos[None, :] <= query_pos[:, None])


def forward_tile(current, queries3, keys3, values3, visible, scale):
    running, total, accum = current
    scores = jnp.einsum("qhd,khd->hqk", queries3, keys3, preferred_element_type=jnp.float32) * scale
    scores = jnp.where(visible[None], scores, -1000000000.0)
    highest = jnp.maximum(running, jnp.max(scores, axis=-1))
    weights = jnp.where(visible[None], jnp.exp(scores - highest[..., None]), 0.0)
    factor = jnp.exp(running - highest)
    total = total * factor + jnp.sum(weights, axis=-1)
    accum = accum * factor[..., None] + jnp.einsum(
        "hqk,khd->hqd", weights.astype(jnp.bfloat16), values3, preferred_element_type=jnp.float32
    )
    return (highest, total, accum)


def attend_forward(query_parts, pos_parts, positions, boundary, keys_group, values_group, key_span):
    heads_local, head_size = (query_parts[0].shape[1], query_parts[0].shape[2])
    scale = head_size ** (-0.5)

    def fold_keys(state, pieces, start):
        key_rows, value_rows = pieces
        count_rows = key_rows.shape[0]
        block_rows = math.gcd(count_rows, key_span)
        block_count = count_rows // block_rows

        def one_step(index, inner):
            offset = index * block_rows
            keys3 = lax.dynamic_slice_in_dim(key_rows, offset, block_rows).reshape(
                block_rows, heads_local, head_size
            )
            values3 = lax.dynamic_slice_in_dim(value_rows, offset, block_rows).reshape(
                block_rows, heads_local, head_size
            )
            key_pos = lax.dynamic_slice_in_dim(positions, offset, block_rows)
            part_queries = query_parts[0]
            visible = visible_pairs(pos_parts[0], key_pos, boundary)
            current = inner[0]
            result = forward_tile(current, part_queries, keys3, values3, visible, scale)
            updated = [result]
            return tuple(updated)

        return lax.fori_loop(0, block_count, one_step, state)

    initial = tuple(
        (
            (
                jnp.full((heads_local, part.shape[0]), -1000000000.0, jnp.float32),
                jnp.zeros((heads_local, part.shape[0]), jnp.float32),
                jnp.zeros((heads_local, part.shape[0], head_size), jnp.float32),
            )
            for part in query_parts
        )
    )
    return fold_keys(
        initial,
        (
            lax.all_gather(keys_group, "blk", axis=0, tiled=True),
            lax.all_gather(values_group, "blk", axis=0, tiled=True),
        ),
        jnp.int32(0),
    )


def backward_tile(current, queries3, grad3, log_total, delta, keys3, values3, visible, scale):
    grad_query, term = current
    scores = jnp.einsum("qhd,khd->hqk", queries3, keys3, preferred_element_type=jnp.float32) * scale
    scores = jnp.where(visible[None], scores, -1000000000.0)
    exact = jnp.where(visible[None], jnp.exp(scores - log_total[..., None]), 0.0)
    grad_probs = jnp.einsum("qhd,khd->hqk", grad3, values3, preferred_element_type=jnp.float32)
    grad_scores = (exact * (grad_probs - delta[..., None])).astype(jnp.bfloat16)
    grad_query = (
        grad_query
        + jnp.einsum("hqk,khd->hqd", grad_scores, keys3, preferred_element_type=jnp.float32) * scale
    )
    rounded = exact.astype(jnp.bfloat16)
    grad_values = jnp.einsum("hqk,qhd->khd", rounded, grad3, preferred_element_type=jnp.float32)
    grad_keys = (
        jnp.einsum("hqk,qhd->khd", grad_scores, queries3, preferred_element_type=jnp.float32)
        * scale
    )
    rows = keys3.shape[0]
    term = jnp.stack([grad_keys.reshape(rows, -1), grad_values.reshape(rows, -1)], axis=1)
    return (grad_query, term)


def attend_backward(
    query_parts,
    grad_parts,
    total_parts,
    delta_parts,
    pos_parts,
    positions,
    boundary,
    keys_group,
    values_group,
    key_span,
    buffer_rows,
):
    heads_local, head_size = (query_parts[0].shape[1], query_parts[0].shape[2])
    scale = head_size ** (-0.5)

    def fold_keys(state, pieces, start):
        key_rows, value_rows = pieces
        count_rows = key_rows.shape[0]
        block_rows = math.gcd(count_rows, key_span)
        block_count = count_rows // block_rows

        def one_step(index, inner):
            offset = index * block_rows
            keys3 = lax.dynamic_slice_in_dim(key_rows, offset, block_rows).reshape(
                block_rows, heads_local, head_size
            )
            values3 = lax.dynamic_slice_in_dim(value_rows, offset, block_rows).reshape(
                block_rows, heads_local, head_size
            )
            key_pos = lax.dynamic_slice_in_dim(positions, offset, block_rows)
            grads_now, buffer = inner
            term = jnp.zeros((block_rows, 2, heads_local * head_size), jnp.float32)
            part_queries = query_parts[0]
            part_grads = grad_parts[0]
            part_total = total_parts[0]
            part_delta = delta_parts[0]
            visible = visible_pairs(pos_parts[0], key_pos, boundary)
            current = (grads_now[0], term)
            result = backward_tile(
                current,
                part_queries,
                part_grads,
                part_total,
                part_delta,
                keys3,
                values3,
                visible,
                scale,
            )
            updated = [result[0]]
            term = result[1]
            buffer = lax.dynamic_update_slice(buffer, term, (offset, 0, 0))
            return (tuple(updated), buffer)

        return lax.fori_loop(0, block_count, one_step, state)

    grads_init = tuple(
        (jnp.zeros((heads_local, part.shape[0], head_size), jnp.float32) for part in query_parts)
    )
    initial = (grads_init, jnp.zeros((buffer_rows, 2, heads_local * head_size), jnp.float32))
    return fold_keys(
        initial,
        (
            lax.all_gather(keys_group, "blk", axis=0, tiled=True),
            lax.all_gather(values_group, "blk", axis=0, tiled=True),
        ),
        jnp.int32(0),
    )


def body(
    block_input,
    qkv_weight,
    q_bias,
    v_bias,
    out_weight,
    out_bias,
    norm1_gain,
    norm1_shift,
    norm2_gain,
    norm2_shift,
    fc_weight,
    fc_bias,
    proj_weight,
    proj_bias,
    out_grad,
    dealt,
    lengths,
):
    micro_count, local_rows, width = block_input.shape
    head_devices = lax.axis_size("head")
    blk_devices = lax.axis_size("blk")
    group = local_rows * head_devices
    blk_index = lax.axis_index("blk")
    head_size = DH
    key_span = 1024
    part_count = group // group
    shards = (
        qkv_weight,
        q_bias,
        v_bias,
        out_weight,
        out_bias,
        norm1_gain,
        norm1_shift,
        norm2_gain,
        norm2_shift,
        fc_weight,
        fc_bias,
        proj_weight,
        proj_bias,
    )
    totals = [
        jnp.zeros((shard.shape[0] * blk_devices * head_devices,) + shard.shape[1:], jnp.float32)
        for shard in shards
    ]
    outputs = []
    input_grads = []
    for micro_index in range(micro_count):
        whole = (
            lax.all_gather(shards[0], ("blk", "head"), axis=0, tiled=True),
            lax.all_gather(shards[1], ("blk", "head"), axis=0, tiled=True),
            lax.all_gather(shards[2], ("blk", "head"), axis=0, tiled=True),
            lax.all_gather(shards[3], ("blk", "head"), axis=0, tiled=True),
            lax.all_gather(shards[4], ("blk", "head"), axis=0, tiled=True),
            lax.all_gather(shards[5], ("blk", "head"), axis=0, tiled=True),
            lax.all_gather(shards[6], ("blk", "head"), axis=0, tiled=True),
            lax.all_gather(shards[7], ("blk", "head"), axis=0, tiled=True),
            lax.all_gather(shards[8], ("blk", "head"), axis=0, tiled=True),
            lax.all_gather(shards[9], ("blk", "head"), axis=0, tiled=True),
            lax.all_gather(shards[10], ("blk", "head"), axis=0, tiled=True),
            lax.all_gather(shards[11], ("blk", "head"), axis=0, tiled=True),
            lax.all_gather(shards[12], ("blk", "head"), axis=0, tiled=True),
        )
        (
            w_qkv,
            b_query,
            b_value,
            w_out,
            b_out,
            gain_one,
            shift_one,
            gain_two,
            shift_two,
            w_fc,
            b_fc,
            w_proj,
            b_proj,
        ) = whole
        b_query = b_query.astype(jnp.float32)
        b_value = b_value.astype(jnp.float32)
        b_out = b_out.astype(jnp.float32)
        gain_one = gain_one.astype(jnp.float32)
        shift_one = shift_one.astype(jnp.float32)
        gain_two = gain_two.astype(jnp.float32)
        shift_two = shift_two.astype(jnp.float32)
        b_fc = b_fc.astype(jnp.float32)
        b_proj = b_proj.astype(jnp.float32)
        positions = dealt[micro_index]
        boundary = lengths[micro_index, 0]
        query_pos = lax.dynamic_slice_in_dim(positions, blk_index * group, group)
        inputs = block_input[micro_index].astype(jnp.float32)
        normed_one, inverse_one = normalize(inputs)
        act_one = (normed_one * gain_one + shift_one).astype(jnp.bfloat16)
        mixed = product(act_one, w_qkv)
        queries = (mixed[:, :width] + b_query).astype(jnp.bfloat16)
        keys = mixed[:, width : 2 * width].astype(jnp.bfloat16)
        values = (mixed[:, 2 * width :] + b_value).astype(jnp.bfloat16)
        heads_in = lax.all_to_all(
            jnp.stack([queries, keys, values], axis=1),
            "head",
            split_axis=2,
            concat_axis=0,
            tiled=True,
        )
        local_width = heads_in.shape[2]
        heads_local = local_width // head_size
        queries3 = heads_in[:, 0].reshape(group, heads_local, head_size)
        keys_group = heads_in[:, 1]
        values_group = heads_in[:, 2]
        query_parts = tuple((queries3 for index in range(part_count)))
        pos_parts = tuple((query_pos for index in range(part_count)))
        states = attend_forward(
            query_parts, pos_parts, positions, boundary, keys_group, values_group, key_span
        )
        running = jnp.concatenate([state[0] for state in states], axis=1)
        total = jnp.concatenate([state[1] for state in states], axis=1)
        accum = jnp.concatenate([state[2] for state in states], axis=1)
        log_total = running + jnp.log(total)
        attn_heads = (
            (accum / total[..., None])
            .transpose(1, 0, 2)
            .reshape(group, local_width)
            .astype(jnp.bfloat16)
        )
        attended = lax.all_to_all(attn_heads, "head", split_axis=0, concat_axis=1, tiled=True)
        resid = inputs + product(attended, w_out) + b_out
        normed_two, inverse_two = normalize(resid)
        act_two = (normed_two * gain_two + shift_two).astype(jnp.bfloat16)
        pre = product(act_two, w_fc) + b_fc
        hidden = gelu_tanh(pre).astype(jnp.bfloat16)
        outputs.append((resid + product(hidden, w_proj) + b_proj).astype(jnp.bfloat16))
        cotangent = out_grad[micro_index]
        grad_proj_w = product_tn(hidden, cotangent)
        grad_proj_b = jnp.sum(cotangent.astype(jnp.float32), axis=0)
        grad_hidden = product_nt(cotangent, w_proj)
        grad_pre = jax.vjp(gelu_tanh, pre)[1](grad_hidden)[0].astype(jnp.bfloat16)
        grad_fc_w = product_tn(act_two, grad_pre)
        grad_fc_b = jnp.sum(grad_pre.astype(jnp.float32), axis=0)
        grad_act_two = product_nt(grad_pre, w_fc)
        grad_gain_two = jnp.sum(grad_act_two * normed_two, axis=0)
        grad_shift_two = jnp.sum(grad_act_two, axis=0)
        grad_resid = cotangent.astype(jnp.float32) + norm_back(
            grad_act_two * gain_two, normed_two, inverse_two
        )
        grad_branch = grad_resid.astype(jnp.bfloat16)
        grad_out_w = product_tn(attended, grad_branch)
        grad_out_b = jnp.sum(grad_branch.astype(jnp.float32), axis=0)
        grad_attn = product_nt(grad_branch, w_out).astype(jnp.bfloat16)
        grad_heads = lax.all_to_all(grad_attn, "head", split_axis=1, concat_axis=0, tiled=True)
        grad3 = grad_heads.reshape(group, heads_local, head_size)
        attn3 = attn_heads.reshape(group, heads_local, head_size)
        delta = jnp.sum(grad3.astype(jnp.float32) * attn3.astype(jnp.float32), axis=-1).T
        grad_parts = tuple((grad3 for index in range(part_count)))
        total_parts = tuple((log_total for index in range(part_count)))
        delta_parts = tuple((delta for index in range(part_count)))
        query_grads, buffer = attend_backward(
            query_parts,
            grad_parts,
            total_parts,
            delta_parts,
            pos_parts,
            positions,
            boundary,
            keys_group,
            values_group,
            key_span,
            group * blk_devices,
        )
        kv_sums = lax.psum_scatter(buffer, "blk", scatter_dimension=0, tiled=True)
        grad_k_heads = kv_sums[:, 0].astype(jnp.bfloat16)
        grad_v_heads = kv_sums[:, 1].astype(jnp.bfloat16)
        grad_query = jnp.concatenate(list(query_grads), axis=1)
        grad_q_heads = (
            grad_query.transpose(1, 0, 2).reshape(group, local_width).astype(jnp.bfloat16)
        )
        grads_heads = jnp.stack([grad_q_heads, grad_k_heads, grad_v_heads], axis=1)
        back_tokens = lax.all_to_all(grads_heads, "head", split_axis=0, concat_axis=2, tiled=True)
        grad_mixed = back_tokens.reshape(local_rows, 3 * width)
        grad_qkv_w = product_tn(act_one, grad_mixed)
        grad_q_b = jnp.sum(back_tokens[:, 0].astype(jnp.float32), axis=0)
        grad_v_b = jnp.sum(back_tokens[:, 2].astype(jnp.float32), axis=0)
        grad_act_one = product_nt(grad_mixed, w_qkv)
        grad_gain_one = jnp.sum(grad_act_one * normed_one, axis=0)
        grad_shift_one = jnp.sum(grad_act_one, axis=0)
        input_grads.append(
            (grad_resid + norm_back(grad_act_one * gain_one, normed_one, inverse_one)).astype(
                jnp.bfloat16
            )
        )
        terms = (
            grad_qkv_w,
            grad_q_b,
            grad_v_b,
            grad_out_w,
            grad_out_b,
            grad_gain_one,
            grad_shift_one,
            grad_gain_two,
            grad_shift_two,
            grad_fc_w,
            grad_fc_b,
            grad_proj_w,
            grad_proj_b,
        )
        totals = [running_sum + term for running_sum, term in zip(totals, terms)]
    final = (
        lax.psum_scatter(totals[0], ("blk", "head"), scatter_dimension=0, tiled=True),
        lax.psum_scatter(totals[1], ("blk", "head"), scatter_dimension=0, tiled=True),
        lax.psum_scatter(totals[2], ("blk", "head"), scatter_dimension=0, tiled=True),
        lax.psum_scatter(totals[3], ("blk", "head"), scatter_dimension=0, tiled=True),
        lax.psum_scatter(totals[4], ("blk", "head"), scatter_dimension=0, tiled=True),
        lax.psum_scatter(totals[5], ("blk", "head"), scatter_dimension=0, tiled=True),
        lax.psum_scatter(totals[6], ("blk", "head"), scatter_dimension=0, tiled=True),
        lax.psum_scatter(totals[7], ("blk", "head"), scatter_dimension=0, tiled=True),
        lax.psum_scatter(totals[8], ("blk", "head"), scatter_dimension=0, tiled=True),
        lax.psum_scatter(totals[9], ("blk", "head"), scatter_dimension=0, tiled=True),
        lax.psum_scatter(totals[10], ("blk", "head"), scatter_dimension=0, tiled=True),
        lax.psum_scatter(totals[11], ("blk", "head"), scatter_dimension=0, tiled=True),
        lax.psum_scatter(totals[12], ("blk", "head"), scatter_dimension=0, tiled=True),
    )
    return (
        jnp.stack(outputs),
        jnp.stack(input_grads),
        final[0],
        final[1],
        final[2],
        final[3],
        final[4],
        final[5],
        final[6],
        final[7],
        final[8],
        final[9],
        final[10],
        final[11],
        final[12],
    )


def solution(mesh):
    in_specs = (
        P(None, ("blk", "head"), None),
        P(("blk", "head"), None),
        P(("blk", "head")),
        P(("blk", "head")),
        P(("blk", "head"), None),
        P(("blk", "head")),
        P(("blk", "head")),
        P(("blk", "head")),
        P(("blk", "head")),
        P(("blk", "head")),
        P(("blk", "head"), None),
        P(("blk", "head")),
        P(("blk", "head"), None),
        P(("blk", "head")),
        P(None, ("blk", "head"), None),
        P(),
        P(),
    )
    out_specs = (
        P(None, ("blk", "head"), None),
        P(None, ("blk", "head"), None),
        P(("blk", "head"), None),
        P(("blk", "head")),
        P(("blk", "head")),
        P(("blk", "head"), None),
        P(("blk", "head")),
        P(("blk", "head")),
        P(("blk", "head")),
        P(("blk", "head")),
        P(("blk", "head")),
        P(("blk", "head"), None),
        P(("blk", "head")),
        P(("blk", "head"), None),
        P(("blk", "head")),
    )
    return jax.shard_map(body, mesh=mesh, in_specs=in_specs, out_specs=out_specs, check_vma=False)
```

profile of v0, /device:TPU:11, one launch (start us, length us, event | category | flops | bytes accessed | tf_op | source)
XLA Modules:
  0.0 2465.0 jit_solution(6141742924274452463)
XLA Ops:
  16.7 40.5 %all-reduce.21 = (bf16[1024]{0:T(1024)(128)(2,1)S(1)}, bf16[1024]{0:T(1024)(128)(2,1)S(1)}, bf16[1024]{0:T(1024)(128)(2,1)S(1)}, bf16[1024]{0:T(1024)(128)(2,1)S...) all-reduce(bf16[1024]{0:T(1024)(128)(2,1)S(1)} %dynamic-update-slic, ...), channel_id=1, replica_groups=mesh['head'=2,'blk'=16] {'blk','head'}, use_global_device_ids=true, to_apply=%add.1 | all-reduce | flops 8192 | bytes 32768
  59.8 22.3 all-gather.14.cloned.1.call-done
  91.5 17.0 all_to_all.136
  117.2 15.3 all_to_all.137
  138.7 50.4 %all-gather.4 = bf16[32,1,128]{2,1,0:T(2,128)(2,1)S(1)} all-gather(bf16[1,1,128]{2,1,0:T(2,128)(2,1)S(1)} %bitcast.482), channel_id=1, replica_groups=mesh['head'=2,'blk'=16] {'blk','head'}, dimensions={0}, use_global_device_ids=true | all-gather | bytes 8448 | tf_op jit(solution)/shard_map/all_gather | solution.py:266
  189.8 29.6 %all-gather.26.cloned.1.call-done = bf16[4096,1,512]{0,2,1:T(8,128)(2,1)} async-done(((bf16[256,1,512]{0,2,1:T(8,128)(2,1)}), bf16[4096,1,512]{0,2,1:T(8,128)(2,1)}) %all-gather.26.cloned.1.call-update) | async-done | bytes 4194320 | tf_op jit(solution)/shard_map/all_gather | solution.py:106
  219.5 36.9 %while.69 = (s32[]{:T(128)}, f32[8,256]{1,0:T(8,128)S(1)}, f32[8,256]{1,0:T(8,128)S(1)}, f32[8,256,64]{1,2,0:T(8,128)S(1)}, s32[]{:T(128)}, /*index=5*/s32[256]{...) while((s32[]{:T(128)}, f32[8,256]{1,0:T(8,128)S(1)}, ...), condition=%wide.region_13.14_spmd.clone, body=%wide.region_10.13_spmd.clone.sunk | while | flops 565325056 | bytes 33964756 | solution.py:91
  257.2 16.2 all-gather.24.cloned.1.call-done
  273.5 53.4 %all-gather.22.cloned.1.call-done = bf16[4096,1,512]{0,2,1:T(8,128)(2,1)} async-done(((bf16[256,1,512]{0,2,1:T(8,128)(2,1)}), bf16[4096,1,512]{0,2,1:T(8,128)(2,1)}) %all-gather.22.cloned.1.call-update) | async-done | bytes 4194320 | tf_op jit(solution)/shard_map/all_gather | solution.py:106
  326.9 36.8 %while.68 = (s32[]{:T(128)}, f32[8,256]{1,0:T(8,128)S(1)}, f32[8,256]{1,0:T(8,128)S(1)}, f32[8,256,64]{1,2,0:T(8,128)S(1)}, s32[]{:T(128)}, /*index=5*/s32[256]{...) while((s32[]{:T(128)}, f32[8,256]{1,0:T(8,128)S(1)}, ...), condition=%wide.region_5.6_spmd.clone, body=%wide.region_2.5_spmd.clone.sunk | while | flops 565325056 | bytes 33964756 | solution.py:91
  377.7 8.7 all-gather.16.cloned.1.call-done
  391.6 75.3 %all-gather.18.cloned.1.call-done = bf16[1024,4096]{1,0:T(8,128)(2,1)} async-done(((bf16[32,4096]{1,0:T(8,128)(2,1)}), bf16[1024,4096]{1,0:T(8,128)(2,1)}) %all-gather.18.cloned.1.call-update) | async-done | bytes 8388624 | tf_op jit(solution)/shard_map/all_gather | solution.py:265
  472.9 73.1 %all-gather.20.cloned.1.call-done = bf16[4096,1024]{1,0:T(8,128)(2,1)} async-done(((bf16[128,1024]{1,0:T(8,128)(2,1)}), bf16[4096,1024]{1,0:T(8,128)(2,1)}) %all-gather.20.cloned.1.call-update) | async-done | bytes 8388624 | tf_op jit(solution)/shard_map/all_gather | solution.py:267
  546.0 8.9 convert_reduce_fusion
  602.8 111.9 %while.71 = (s32[]{:T(128)}, f32[8,256,64]{1,2,0:T(8,128)S(1)}, f32[4096,2,512]{2,1,0:T(2,128)}, s32[]{:T(128)}, s32[256]{0:T(256)S(1)}, /*index=5*/s32[4096]{0:...) while((s32[]{:T(128)}, f32[8,256,64]{1,2,0:T(8,128)S(1)}, ...), condition=%wide.region_28.0_spmd.clone, body=%wide.region_27.28_spmd.clone.sunk | while | flops 1370096896 | bytes 77374184 | solution.py:190
  721.4 114.8 %while.70 = (s32[]{:T(128)}, f32[8,256,64]{1,2,0:T(8,128)S(1)}, f32[4096,2,512]{2,1,0:T(2,128)}, s32[]{:T(128)}, s32[256]{0:T(256)S(1)}, /*index=5*/s32[4096]{0:...) while((s32[]{:T(128)}, f32[8,256,64]{1,2,0:T(8,128)S(1)}, ...), condition=%wide.region_20.21_spmd.clone, body=%wide.region_19.20_spmd.clone.sunk | while | flops 1370096896 | bytes 77374184 | solution.py:190
  836.3 684.5 %all-reduce.23 = (bf16[4096,2,512]{2,1,0:T(2,128)(2,1)}, bf16[4096,2,512]{2,1,0:T(2,128)(2,1)}) all-reduce(f32[4096,2,512]{2,1,0:T(2,128)} %get-tuple-element.766, f32[4096,2,512]{2,1,0:T(2,128)} %get-tuple-element.763), channel_id=7, replica_groups=mesh['head'=2,'blk'=16] {'blk'}, use_global_device_ids=true, to_apply=%region_29.0.clone | all-reduce | flops 8388608 | bytes 50331648
  1542.4 10.1 all-to-all-done.5
  1567.8 9.2 convolution_add_fusion
  1581.8 8.8 convolution_add_fusion.1
  1610.2 63.4 %all-reduce.19 = (f32[1024]{0:T(1024)S(1)}, f32[1024]{0:T(1024)S(1)}, f32[1024]{0:T(1024)S(1)}, f32[1024]{0:T(1024)S(1)}, f32[1024]{0:T(1024)S(1)}, /*index=5*/f...) all-reduce(f32[1024]{0:T(1024)S(1)} %add.447, ...), channel_id=9, replica_groups=mesh['head'=2,'blk'=16] {'blk','head'}, use_global_device_ids=true, to_apply=%region_35.36.clone | all-reduce | flops 12288 | bytes 98304
  1680.3 55.1 %reduce-scatter.5.cloned.1.call-done = f32[32,3072]{1,0:T(8,128)} async-done(((f32[1024,3072]{1,0:T(8,128)}), f32[32,3072]{1,0:T(8,128)}) %reduce-scatter.5.cloned.1.call-update) | async-done | bytes 393232 | tf_op jit(solution)/shard_map/reduce_scatter | solution.py:413
  1735.4 361.1 %reduce-scatter.11.cloned.1.call-done = f32[128,1024]{1,0:T(8,128)} async-done(((f32[4096,1024]{1,0:T(8,128)}), f32[128,1024]{1,0:T(8,128)}) %reduce-scatter.11.cloned.1.call-update) | async-done | bytes 524304 | tf_op jit(solution)/shard_map/reduce_scatter | solution.py:424
  2096.4 361.3 %reduce-scatter.9.cloned.1.call-done = f32[32,4096]{1,0:T(8,128)} async-done(((f32[1024,4096]{1,0:T(8,128)}), f32[32,4096]{1,0:T(8,128)}) %reduce-scatter.9.cloned.1.call-update) | async-done | bytes 524304 | tf_op jit(solution)/shard_map/reduce_scatter | solution.py:422
  (525 shorter events, 480.3 us)
Async XLA Ops:
  7.2 74.9 %all-gather.14.cloned.1.call-start = ((), (), s32[]{:S(2)}) async-start(), calls=%async_computation.12 | async-start | bytes 6488064 | tf_op jit(solution)/shard_map/all_gather | solution.py:256
  7.9 181.9 %all-gather.28.cloned.1.call-start = ((), (), s32[]{:S(2)}) async-start(), calls=%async_computation.23 | async-start | bytes 4456448 | tf_op jit(solution)/shard_map/all_gather | solution.py:107
  115.5 104.0 %all-gather.26.cloned.1.call-start = ((), (), s32[]{:S(2)}) async-start(), calls=%async_computation.22 | async-start | bytes 4456448 | tf_op jit(solution)/shard_map/all_gather | solution.py:106
  116.2 157.2 %all-gather.24.cloned.1.call-start = ((), (), s32[]{:S(2)}) async-start(), calls=%async_computation.21 | async-start | bytes 4456448 | tf_op jit(solution)/shard_map/all_gather | solution.py:107
  134.8 192.1 %all-gather.22.cloned.1.call-start = ((), (), s32[]{:S(2)}) async-start(), calls=%async_computation.20 | async-start | bytes 4456448 | tf_op jit(solution)/shard_map/all_gather | solution.py:106
  135.4 251.1 %all-gather.16.cloned.1.call-start = ((), (), s32[]{:S(2)}) async-start(), calls=%async_computation.13 | async-start | bytes 2162688 | tf_op jit(solution)/shard_map/all_gather | solution.py:259
  136.0 330.9 %all-gather.18.cloned.1.call-start = ((), (), s32[]{:S(2)}) async-start(), calls=%async_computation.14 | async-start | bytes 8650752 | tf_op jit(solution)/shard_map/all_gather | solution.py:265
  136.7 409.3 %all-gather.20.cloned.1.call-start = ((), (), s32[]{:S(2)}) async-start(), calls=%async_computation.15 | async-start | bytes 8650752 | tf_op jit(solution)/shard_map/all_gather | solution.py:267
  138.7 431.4 %copy-start.33 = (f32[1024]{0:T(1024)}, f32[1024]{0:T(1024)S(1)}, u32[]{:S(2)}) copy-start(f32[1024]{0:T(1024)S(1)} %convert_element_type.291) | copy-start | bytes 12292
  138.7 420.2 %copy-start.35 = (f32[1024]{0:T(1024)}, f32[1024]{0:T(1024)S(1)}, u32[]{:S(2)}) copy-start(f32[1024]{0:T(1024)S(1)} %convert_element_type.292) | copy-start | bytes 12292
  364.7 8.5 all-to-all-start.1
  373.2 16.5 all-to-all-start.3
  388.7 181.3 %copy-start.47 = (f32[128]{0:T(128)}, f32[128]{0:T(128)S(1)}, u32[]{:S(2)}) copy-start(f32[128]{0:T(128)S(1)} %broadcast_multiply_fusion.10) | copy-start | bytes 1540
  391.3 178.7 %copy-start.5 = (f32[128,1024]{1,0:T(8,128)}, f32[128,1024]{1,0:T(8,128)S(1)}, u32[]{:S(2)}) copy-start(f32[128,1024]{1,0:T(8,128)S(1)} %get-tuple-element.1129) | copy-start | bytes 1572868
  391.4 178.7 %copy-start.49 = (f32[128]{0:T(128)}, f32[128]{0:T(128)S(1)}, u32[]{:S(2)}) copy-start(f32[128]{0:T(128)S(1)} %broadcast_multiply_fusion.8) | copy-start | bytes 1540
  391.6 178.5 %copy-start.57 = (f32[128]{0:T(128)}, f32[128]{0:T(128)S(1)}, u32[]{:S(2)}) copy-start(f32[128]{0:T(128)S(1)} %add_rsqrt_fusion.2) | copy-start | bytes 1540
  574.4 11.6 all-to-all-start.6
  577.8 1102.4 %reduce-scatter.7.cloned.1.call-start = ((), (), s32[]{:S(2)}) async-start(), calls=%async_computation.17 | async-start | bytes 4325376 | tf_op jit(solution)/shard_map/reduce_scatter | solution.py:416
  586.0 10.0 all-to-all-start.4
  1524.3 11.8 all-to-all-start.7
  1536.1 16.3 all-to-all-start.5
  1539.7 195.7 %reduce-scatter.5.cloned.1.call-start = ((), (), s32[]{:S(2)}) async-start(), calls=%async_computation.16 | async-start | bytes 12976128 | tf_op jit(solution)/shard_map/reduce_scatter | solution.py:413
  1563.7 532.8 %reduce-scatter.11.cloned.1.call-start = ((), (), s32[]{:S(2)}) async-start(), calls=%async_computation.19 | async-start | bytes 17301504 | tf_op jit(solution)/shard_map/reduce_scatter | solution.py:424
  1577.1 880.6 %reduce-scatter.9.cloned.1.call-start = ((), (), s32[]{:S(2)}) async-start(), calls=%async_computation.18 | async-start | bytes 17301504 | tf_op jit(solution)/shard_map/reduce_scatter | solution.py:422
  (76 other events, 1116.5 us)
Sparse Core Ops, SparseCore 0:
  10.9 71.1 all-gather.13
  115.6 49.6 all-gather.27
  168.0 51.4 all-gather.25
  222.0 51.3 all-gather.23
  275.5 51.3 all-gather.21
  329.9 56.5 all-gather.15
  389.5 77.2 all-gather.17
  470.0 75.9 all-gather.19
  586.1 119.1 reduce-scatter.6
  1563.8 171.5 reduce-scatter.4
  1738.4 358.0 reduce-scatter.10
  2099.3 358.4 reduce-scatter.8
where the time goes:
time: 2480 us; the launch traced here: 2460 us
  waiting for transfers between devices  1080 us (44%)
  blocking collectives  871 us (35%)
  matrix products  200 us (8%)
  local copies, waits for them, and re-layouts  188 us (8%)
  other arithmetic  78.6 us (3%)
    unnamed x3, blocking collectives  788 us
    reduce_scatter x1, waiting for transfers between devices, body(): lax.psum_scatter(totals[9], ('blk', 'head'), scatter_dimension=0, tiled=T...  361 us
    reduce_scatter x1, waiting for transfers between devices, body(): lax.psum_scatter(totals[11], ('blk', 'head'), scatter_dimension=0, tiled=...  361 us
    dynamic_update_slice x16, local copies, waits for them, and re-layouts, one_step(): buffer = lax.dynamic_update_slice(buffer, term, (offset, 0, 0))  103 us
    all_gather x2, waiting for transfers between devices, attend_forward(): lax.all_gather(keys_group, 'blk', axis=0, tiled=True)  83 us
    all_gather x1, waiting for transfers between devices, body(): lax.all_gather(shards[9], ('blk', 'head'), axis=0, tiled=True)  75.3 us
    all_gather x1, waiting for transfers between devices, body(): lax.all_gather(shards[11], ('blk', 'head'), axis=0, tiled=True)  73.1 us
    reduce_scatter x1, waiting for transfers between devices, body(): lax.psum_scatter(totals[0], ('blk', 'head'), scatter_dimension=0, tiled=T...  55.1 us
  transfers between devices with their start and end apart: 18, of which 14 were waited for; matrix products, arithmetic and copies ran while one was open for 17% of the time, Pallas kernels for 0%

commit v1 on v0

--- a/solution.py
+++ b/solution.py
@@ -1,8 +1,12 @@
+import functools
 import math
 
 import jax
 import jax.numpy as jnp
 from jax import lax
+from jax.experimental import pallas as pl
+from jax.experimental.pallas import tpu as pltpu
+from jax.sharding import Mesh
 from jax.sharding import PartitionSpec as P
 
 DH = 64
@@ -62,7 +66,7 @@
     return (highest, total, accum)
 
 
-def attend_forward(query_parts, pos_parts, positions, boundary, keys_group, values_group, key_span):
+def general_forward(query_parts, pos_parts, positions, boundary, keys_group, values_group, key_span):
     heads_local, head_size = (query_parts[0].shape[1], query_parts[0].shape[2])
     scale = head_size ** (-0.5)
 
@@ -132,7 +136,7 @@
     return (grad_query, term)
 
 
-def attend_backward(
+def general_backward(
     query_parts,
     grad_parts,
     total_parts,
@@ -203,7 +207,7 @@
     )
 
 
-def body(
+def general_body(
     block_input,
     qkv_weight,
     q_bias,
@@ -315,7 +319,7 @@
         values_group = heads_in[:, 2]
         query_parts = tuple((queries3 for index in range(part_count)))
         pos_parts = tuple((query_pos for index in range(part_count)))
-        states = attend_forward(
+        states = general_forward(
             query_parts, pos_parts, positions, boundary, keys_group, values_group, key_span
         )
         running = jnp.concatenate([state[0] for state in states], axis=1)
@@ -359,7 +363,7 @@
         grad_parts = tuple((grad3 for index in range(part_count)))
         total_parts = tuple((log_total for index in range(part_count)))
         delta_parts = tuple((delta for index in range(part_count)))
-        query_grads, buffer = attend_backward(
+        query_grads, buffer = general_backward(
             query_parts,
             grad_parts,
             total_parts,
@@ -443,41 +447,534 @@
     )
 
 
+RUN = 64
+BLOCK = 512
+NEG = -1000000000.0
+VM = pltpu.VMEM
+SM = pltpu.SMEM
+
+
+def dot_nt(left, right):
+    return lax.dot_general(left, right, (((1,), (1,)), ((), ())), preferred_element_type=jnp.float32)
+
+
+def dot_nn(left, right):
+    return lax.dot_general(left, right, (((1,), (0,)), ((), ())), preferred_element_type=jnp.float32)
+
+
+def rows_at(index, size):
+    return pl.ds(pl.multiple_of(index * size, size), size)
+
+
+def first_block(start, bound):
+    return jnp.where(start >= bound, bound // BLOCK, 0)
+
+
+def forward_kernel(head_size, bound_ref, inloc, outloc, qkv, out, qs, ks, vs, attn_t, lse, vt, mixed):
+    tokens = qkv.shape[0]
+    runs = tokens // RUN
+    scale = head_size ** (-0.5)
+    bound = bound_ref[0]
+
+    @pl.loop(0, runs)
+    def _(run):
+        rows = qkv[rows_at(inloc[run], RUN), :]
+        here = rows_at(run, RUN)
+        qs[here, :] = (rows[:, :head_size].astype(jnp.float32) * scale).astype(jnp.bfloat16)
+        ks[here, :] = rows[:, head_size : 2 * head_size]
+        vs[here, :] = rows[:, 2 * head_size :]
+
+    @pl.loop(0, tokens // BLOCK)
+    def _(block):
+        here = rows_at(block, BLOCK)
+        vt[:, here] = vs[here, :].astype(jnp.float32).T.astype(jnp.bfloat16)
+
+    @pl.loop(0, tokens // BLOCK)
+    def _(block):
+        start = block * BLOCK
+        here = rows_at(block, BLOCK)
+        queries = qs[here, :]
+        query_pos = start + lax.broadcasted_iota(jnp.int32, (1, BLOCK), 1)
+        floor = jnp.where(query_pos >= bound, bound, 0)
+
+        def scores_of(index, diagonal):
+            keys = ks[rows_at(index, BLOCK), :]
+            scores = dot_nt(keys, queries)
+            key_pos = index * BLOCK + lax.broadcasted_iota(jnp.int32, (BLOCK, BLOCK), 0)
+            visible = key_pos >= floor
+            if diagonal:
+                visible = visible & (key_pos <= query_pos)
+            return jnp.where(visible, scores, NEG)
+
+        scores = scores_of(block, True)
+        highest = jnp.max(scores, axis=0, keepdims=True)
+        weights = jnp.exp(scores - highest)
+        total = jnp.sum(weights, axis=0, keepdims=True)
+        accum = dot_nn(vt[:, here], weights.astype(jnp.bfloat16))
+
+        def step(index, state):
+            highest, total, accum = state
+            scores = scores_of(index, False)
+            higher = jnp.maximum(highest, jnp.max(scores, axis=0, keepdims=True))
+            weights = jnp.exp(scores - higher)
+            factor = jnp.exp(highest - higher)
+            total = total * factor + jnp.sum(weights, axis=0, keepdims=True)
+            accum = accum * factor + dot_nn(vt[:, rows_at(index, BLOCK)], weights.astype(jnp.bfloat16))
+            return higher, total, accum
+
+        highest, total, accum = lax.fori_loop(first_block(start, bound), block, step, (highest, total, accum))
+        result = accum / total
+        attn_t[:, here] = result.astype(jnp.bfloat16)
+        lse[:, here] = highest + jnp.log(total)
+        result = result.T.astype(jnp.bfloat16)
+        for part in range(BLOCK // RUN):
+            mixed[rows_at(outloc[block * (BLOCK // RUN) + part], RUN), :] = result[part * RUN : (part + 1) * RUN]
+
+    chips, _, span = out.shape
+
+    @pl.loop(0, chips)
+    def _(chip):
+        out[chip] = mixed[rows_at(chip, span), :].astype(jnp.float32).T.astype(jnp.bfloat16)
+
+
+def attend_forward(bound, inloc, outloc, qkv, chips, head_size):
+    tokens = qkv.shape[0]
+    bf16 = jnp.bfloat16
+    pairs = tokens * (tokens // 2)
+    return pl.pallas_call(
+        functools.partial(forward_kernel, head_size),
+        out_shape=(
+            jax.ShapeDtypeStruct((chips, head_size, tokens // chips), bf16),
+            jax.ShapeDtypeStruct((tokens, head_size), bf16),
+            jax.ShapeDtypeStruct((tokens, head_size), bf16),
+            jax.ShapeDtypeStruct((tokens, head_size), bf16),
+            jax.ShapeDtypeStruct((head_size, tokens), bf16),
+            jax.ShapeDtypeStruct((1, tokens), jnp.float32),
+        ),
+        in_specs=[pl.BlockSpec(memory_space=SM)] * 3 + [pl.BlockSpec(memory_space=VM)],
+        out_specs=[pl.BlockSpec(memory_space=VM)] * 6,
+        scratch_shapes=[VM((head_size, tokens), bf16), VM((tokens, head_size), bf16)],
+        compiler_params=pltpu.CompilerParams(vmem_limit_bytes=40 * 1024 * 1024),
+        cost_estimate=pl.CostEstimate(flops=4 * 4 * pairs * head_size, bytes_accessed=tokens * 2048, transcendentals=pairs),
+        name="attend_forward",
+    )(bound, inloc, outloc, qkv)
+
+
+def backward_kernel(
+    head_size, bound_ref, inloc, outloc, grad_t, qs, ks, vs, attn_t, lse, slot_out, send_out, grads, kt, dk, dv, mixed, wide, moved
+):
+    tokens = qs.shape[0]
+    runs = tokens // RUN
+    scale = head_size ** (-0.5)
+    bound = bound_ref[0]
+    chips, _, span = grad_t.shape
+
+    @pl.loop(0, chips)
+    def _(chip):
+        mixed[rows_at(chip, span), :] = grad_t[chip].astype(jnp.float32).T.astype(jnp.bfloat16)
+
+    @pl.loop(0, runs)
+    def _(run):
+        grads[rows_at(run, RUN), :] = mixed[rows_at(outloc[run], RUN), :]
+
+    @pl.loop(0, tokens // BLOCK)
+    def _(block):
+        here = rows_at(block, BLOCK)
+        kt[:, here] = ks[here, :].astype(jnp.float32).T.astype(jnp.bfloat16)
+
+    @pl.loop(0, tokens // BLOCK)
+    def _(block):
+        start = block * BLOCK
+        here = rows_at(block, BLOCK)
+        queries = qs[here, :]
+        grad = grads[here, :]
+        log_total = lse[:, here]
+        delta = jnp.sum(grad.astype(jnp.float32).T * attn_t[:, here].astype(jnp.float32), axis=0, keepdims=True)
+        query_pos = start + lax.broadcasted_iota(jnp.int32, (1, BLOCK), 1)
+        floor = jnp.where(query_pos >= bound, bound, 0)
+
+        def one(index, diagonal):
+            there = rows_at(index, BLOCK)
+            scores = dot_nt(ks[there, :], queries)
+            key_pos = index * BLOCK + lax.broadcasted_iota(jnp.int32, (BLOCK, BLOCK), 0)
+            visible = key_pos >= floor
+            if diagonal:
+                visible = visible & (key_pos <= query_pos)
+            probs = jnp.where(visible, jnp.exp(scores - log_total), 0.0)
+            grad_probs = dot_nt(vs[there, :], grad)
+            grad_scores = (probs * (grad_probs - delta)).astype(jnp.bfloat16)
+            return (
+                dot_nn(probs.astype(jnp.bfloat16), grad),
+                dot_nn(grad_scores, queries),
+                dot_nn(kt[:, there], grad_scores),
+                there,
+            )
+
+        grad_v, grad_k, grad_q, there = one(block, True)
+        dv[there, :] = grad_v
+        dk[there, :] = grad_k
+
+        def step(index, grad_q):
+            grad_v, grad_k, term, there = one(index, False)
+            dv[there, :] += grad_v
+            dk[there, :] += grad_k
+            return grad_q + term
+
+        grad_q = lax.fori_loop(first_block(start, bound), block, step, grad_q)
+        wide[here, :head_size] = (grad_q.T * scale).astype(jnp.bfloat16)
+
+    wide[:, head_size : 2 * head_size] = dk[...].astype(jnp.bfloat16)
+    wide[:, 2 * head_size :] = dv[...].astype(jnp.bfloat16)
+
+    @pl.loop(0, runs)
+    def _(run):
+        slot_out[rows_at(inloc[run], RUN), :] = wide[rows_at(run, RUN), :]
+
+    @pl.loop(0, runs)
+    def _(run):
+        moved[rows_at(outloc[run], RUN), :] = wide[rows_at(run, RUN), :]
+
+    @pl.loop(0, chips)
+    def _(chip):
+        send_out[chip] = moved[rows_at(chip, span), :].astype(jnp.float32).T.astype(jnp.bfloat16)
+
+
+def attend_backward(bound, inloc, outloc, grad_t, qs, ks, vs, attn_t, lse):
+    tokens, head_size = qs.shape
+    chips = grad_t.shape[0]
+    bf16 = jnp.bfloat16
+    pairs = tokens * (tokens // 2)
+    return pl.pallas_call(
+        functools.partial(backward_kernel, head_size),
+        out_shape=(
+            jax.ShapeDtypeStruct((tokens, 3 * head_size), bf16),
+            jax.ShapeDtypeStruct((chips, 3 * head_size, tokens // chips), bf16),
+        ),
+        in_specs=[pl.BlockSpec(memory_space=SM)] * 3 + [pl.BlockSpec(memory_space=VM)] * 6,
+        out_specs=[pl.BlockSpec(memory_space=VM)] * 2,
+        scratch_shapes=[
+            VM((tokens, head_size), bf16),
+            VM((head_size, tokens), bf16),
+            VM((tokens, head_size), jnp.float32),
+            VM((tokens, head_size), jnp.float32),
+            VM((tokens, head_size), bf16),
+            VM((tokens, 3 * head_size), bf16),
+            VM((tokens, 3 * head_size), bf16),
+        ],
+        compiler_params=pltpu.CompilerParams(vmem_limit_bytes=48 * 1024 * 1024),
+        cost_estimate=pl.CostEstimate(flops=4 * 10 * pairs * head_size, bytes_accessed=tokens * 4096, transcendentals=pairs),
+        name="attend_backward",
+    )(bound, inloc, outloc, grad_t, qs, ks, vs, attn_t, lse)
+
+
+PAIR = [(0, 1), (1, 0)]
+
+
+def swap(values, axis):
+    return lax.ppermute(values, axis, PAIR)
+
+
+def in_order(mine, other, index, axis):
+    first = jnp.where(index == 0, mine, other)
+    second = jnp.where(index == 0, other, mine)
+    return jnp.stack([first, second], axis=axis)
+
+
+def shifted(values, count):
+    return [
+        lax.ppermute(values, "z", [(i, (i + step) % count) for i in range(count)]) for step in range(1, count)
+    ]
+
+
+def split_float(values):
+    high = values.astype(jnp.bfloat16)
+    low = (values - high.astype(jnp.float32)).astype(jnp.bfloat16)
+    return high, low
+
+
+def run_table(order, pair_start):
+    pairs = order.shape[0]
+    runs = jnp.arange(2 * pairs, dtype=jnp.int32)[:, None]
+    low = jnp.where(runs == order[None, :], pair_start[None, :], 0)
+    high = jnp.where(runs == 2 * pairs - 1 - order[None, :], pair_start[None, :] + 1, 0)
+    return jnp.sum(low + high, axis=1).astype(jnp.int32)
+
+
+def fast_body(
+    block_input,
+    qkv_weight,
+    q_bias,
+    v_bias,
+    out_weight,
+    out_bias,
+    norm1_gain,
+    norm1_shift,
+    norm2_gain,
+    norm2_shift,
+    fc_weight,
+    fc_bias,
+    proj_weight,
+    proj_bias,
+    out_grad,
+    dealt,
+    lengths,
+):
+    f32, bf16 = jnp.float32, jnp.bfloat16
+    micro, rows, width = block_input.shape
+    nz, nx = lax.axis_size("z"), lax.axis_size("x")
+    iz, ix, ic, iy = (lax.axis_index(name) for name in ("z", "x", "core", "head"))
+    zx = nz * nx
+    every, chips = ("z", "x", "core", "head"), ("z", "x", "head")
+    devices, chip_count = 4 * zx, 2 * zx
+    heads = 2 * zx
+    local = heads * DH // 2
+    share = qkv_weight.shape[0]
+    hidden_share = proj_weight.shape[0]
+    hidden_half = hidden_share * chip_count
+
+    inputs = block_input.astype(f32)
+    normed_one, inverse_one = normalize(inputs)
+    n1 = normed_one.astype(bf16)
+    gain_one = norm1_gain.astype(f32)
+    shift_one = norm1_shift.astype(f32)
+    raw_qkv = qkv_weight.astype(f32)
+    scaled_qkv = (raw_qkv * gain_one[:, None]).astype(bf16)
+    device = ((iz * nx + ix) * 2 + ic) * 2 + iy
+    offset = jnp.sum(raw_qkv * shift_one[:, None], axis=0)
+    zero = jnp.zeros((width,), f32)
+    place = device * share
+    offset = offset + jnp.concatenate(
+        [
+            lax.dynamic_update_slice(zero, q_bias.astype(f32), (place,)),
+            zero,
+            lax.dynamic_update_slice(zero, v_bias.astype(f32), (place,)),
+        ]
+    )
+    high, low = split_float(offset)
+    to_heads = jnp.concatenate([scaled_qkv, high[None], low[None], jnp.zeros((6, 3 * width), bf16)], axis=0)
+    to_heads = to_heads.reshape(share + 8, 3, heads, DH).transpose(2, 0, 1, 3).reshape(heads, 1, share + 8, 3 * DH)
+    to_heads = jnp.broadcast_to(to_heads, (heads, 2, share + 8, 3 * DH)).reshape(devices, share + 8, 3 * DH)
+    head_rows = lax.all_to_all(to_heads, every, split_axis=0, concat_axis=0, tiled=True)
+    head_weight = head_rows[:, :share].reshape(width, 3 * DH)
+    head_offset = jnp.sum(head_rows[:, share : share + 2].astype(f32), axis=(0, 1))
+
+    near = lax.dynamic_index_in_dim(n1, iy, 0, keepdims=False)
+    far = swap(lax.dynamic_index_in_dim(n1, 1 - iy, 0, keepdims=False), "head")
+    a_z = jnp.stack([near] + shifted(near, nz))
+    a_x = swap(a_z, "x")
+    b_x = jnp.stack([far, swap(far, "x")])
+    b_z = [b_x] + shifted(b_x, nz)
+    pieces, owners = [], []
+
+    def add(piece, dz, dx, dy):
+        pieces.append(piece.reshape(-1, width))
+        owners.append((dz, dx, dy))
+
+    def add_all(flip):
+        pick = (lambda v: swap(v, "core")) if flip else (lambda v: v)
+        core = 1 - ic if flip else ic
+        for dx, part in enumerate((a_z, a_x)):
+            pieces.append(pick(part).reshape(-1, width))
+            owners.extend((dz, dx, core, 0) for dz in range(nz))
+        for dz, part in enumerate(b_z):
+            pieces.append(pick(part).reshape(-1, width))
+            owners.extend((dz, dx, core, 1) for dx in range(nx))
+
+    add_all(False)
+    add_all(True)
+    slot_device = jnp.stack(
+        [
+            (((iz - dz) % nz * nx + (ix + dx) % nx) * 2 + core) * 2 + (iy + dy) % 2
+            for dz, dx, core, dy in owners
+        ]
+    ).astype(jnp.int32)
+    my_dealt = lax.dynamic_index_in_dim(dealt, iy, 0, keepdims=False)
+    order = my_dealt.reshape(devices, rows)[:, 0] // RUN
+    slot_of = jnp.sum(
+        jnp.where(jnp.arange(devices)[:, None] == slot_device[None, :], jnp.arange(devices)[None, :], 0), axis=1
+    )
+    inloc = run_table(order, (slot_of * 2).astype(jnp.int32))
+    ids = jnp.arange(devices, dtype=jnp.int32)
+    id_y, id_c, id_zx = ids % 2, ids // 2 % 2, ids // 4
+    send_pair = (id_zx * 2 + id_y) * 2 + (id_c ^ ic)
+    outloc = run_table(order, (send_pair * 2).astype(jnp.int32))
+    bound = lax.dynamic_index_in_dim(lengths, iy, 0, keepdims=False)[:1]
+
+    fc_parts = fc_weight.reshape(share, zx, 2, 2, hidden_share)
+
+    def core_columns(values, index):
+        return lax.dynamic_index_in_dim(values, index, 2, keepdims=False)
+
+    fc_mine = core_columns(fc_parts, ic).reshape(share, hidden_half)
+    fc_other = swap(core_columns(fc_parts, 1 - ic).reshape(share, hidden_half), "core")
+    fc_pair = in_order(fc_mine, fc_other, ic, 0).reshape(2 * share, hidden_half)
+    small = jnp.stack([norm2_gain, norm2_shift, out_bias, proj_bias])
+    small_pair = in_order(small, swap(small, "core"), ic, 0).reshape(8 * share)
+    small_row = jnp.concatenate(
+        [small_pair, fc_bias, jnp.zeros((8 * width - 8 * share - hidden_share,), bf16)]
+    ).reshape(8, width)
+    folds = hidden_half // width
+    fc_folded = fc_pair.reshape(2 * share, folds, width).transpose(1, 0, 2).reshape(-1, width)
+    packed = jnp.concatenate([out_weight, proj_weight, fc_folded, small_row], axis=0)
+    gathered = lax.all_gather(packed, chips, axis=0)
+    out_rows = share
+    proj_rows = hidden_share
+    fc_rows = 2 * share * folds
+    w_out = gathered[:, :out_rows].reshape(local, width)
+    w_proj = gathered[:, out_rows : out_rows + proj_rows].reshape(hidden_half, width)
+    w_fc = gathered[:, out_rows + proj_rows : out_rows + proj_rows + fc_rows]
+    w_fc = w_fc.reshape(zx, 2, folds, 2, share, width).transpose(0, 3, 1, 4, 2, 5).reshape(width, hidden_half)
+    smalls = gathered[:, out_rows + proj_rows + fc_rows :].reshape(chip_count, 8 * width)
+    vectors = smalls[:, : 8 * share].astype(f32).reshape(zx, 2, 2, 4, share)
+    vectors = vectors.transpose(3, 0, 2, 1, 4).reshape(4, width)
+    gain_two, shift_two, b_out, b_proj = vectors[0], vectors[1], vectors[2], vectors[3]
+    b_fc = smalls[:, 8 * share : 8 * share + hidden_share].astype(f32).reshape(hidden_half)
+
+    qkv_parts = scaled_qkv.reshape(share, 3, zx, 2, DH).transpose(0, 2, 1, 3, 4)
+
+    def core_heads(index):
+        return lax.dynamic_index_in_dim(qkv_parts, index, 3, keepdims=False).reshape(share, 3 * local)
+
+    qkv_pair = in_order(core_heads(ic), swap(core_heads(1 - ic), "core"), ic, 0)
+    packed_qkv, gathered, head_rows = lax.optimization_barrier((qkv_pair, gathered, head_rows))
+    w_qkv = lax.all_gather(packed_qkv, chips, axis=0)
+    w_qkv = w_qkv.reshape(zx, 2, 2, share, 3 * local).transpose(0, 2, 1, 3, 4).reshape(width, 3 * local)
+
+    mixed = [(product(piece, head_weight) + head_offset).astype(bf16) for piece in pieces]
+    slots = jnp.concatenate(mixed, axis=0)
+    attn_send, queries, keys, values, attn_t, lse = attend_forward(bound, inloc, outloc, slots, chip_count, DH)
+
+    x_all = jnp.stack([block_input, swap(block_input, "core")]).reshape(-1, width)
+    g_all = jnp.stack([out_grad, swap(out_grad, "core")]).reshape(-1, width)
+    own = micro * rows
+    grad_hidden = product_nt(g_all, w_proj)
+
+    attn_got = lax.all_to_all(attn_send, chips, split_axis=0, concat_axis=0, tiled=True)
+    attn_in = attn_got.reshape(zx, 2, DH, 2, rows).transpose(0, 2, 3, 1, 4).reshape(local, 2 * own)
+
+    def share_sum(part):
+        sent = part.astype(bf16)
+        first = swap(sent[own:], "core")
+        second = swap(sent[:own], "core")
+        return part + jnp.concatenate([first, second], axis=0).astype(f32)
+
+    resid = x_all.astype(f32) + share_sum(product_tn(attn_in, w_out)) + b_out
+    normed_two, inverse_two = normalize(resid)
+    act_two = (normed_two * gain_two + shift_two).astype(bf16)
+    pre = product(act_two, w_fc) + b_fc
+    hidden, gelu_back = jax.vjp(gelu_tanh, pre)
+    hidden = hidden.astype(bf16)
+    projected = product(hidden, w_proj)
+    project_other = swap(projected[own:].astype(bf16), "core")
+    output = (resid[:own] + projected[:own] + project_other.astype(f32) + b_proj).astype(bf16)
+
+    grad_pre = gelu_back(grad_hidden)[0].astype(bf16)
+    grad_proj_w = product_tn(hidden, g_all).astype(bf16)
+    grad_fc_w = product_tn(act_two, grad_pre).astype(bf16)
+    grad_fc_b = jnp.sum(grad_pre.astype(f32), axis=0)
+    grad_proj_b = jnp.sum(g_all.astype(f32), axis=0)
+    grad_act_two = share_sum(product_nt(grad_pre, w_fc))
+    grad_gain_two = jnp.sum(grad_act_two * normed_two, axis=0)
+    grad_shift_two = jnp.sum(grad_act_two, axis=0)
+    grad_resid = g_all.astype(f32) + norm_back(grad_act_two * gain_two, normed_two, inverse_two)
+    grad_branch = grad_resid.astype(bf16)
+    grad_out_b = jnp.sum(grad_branch.astype(f32), axis=0)
+    grad_out_w = product(attn_in, grad_branch).astype(bf16)
+    grad_attn = product_nt(w_out, grad_branch).astype(bf16)
+
+    sums = jnp.stack([grad_gain_two, grad_shift_two, grad_out_b, grad_proj_b]).reshape(4, zx, 2, 2, share)
+    sums = lax.dynamic_index_in_dim(sums, ic, 2, keepdims=False).transpose(1, 2, 0, 3).reshape(chip_count, 4 * share)
+    sums = jnp.concatenate([sums, grad_fc_b.reshape(chip_count, hidden_share)], axis=1)
+    high, low = split_float(sums)
+    extra = jnp.stack([high, low], axis=1)
+    extra = jnp.pad(extra, ((0, 0), (0, 6), (0, 2 * rows - extra.shape[2])))
+    grad_send = grad_attn.reshape(zx, DH, 2, 2, rows).transpose(0, 3, 1, 2, 4).reshape(chip_count, DH, 2 * rows)
+    grad_got = lax.all_to_all(
+        jnp.concatenate([grad_send, extra], axis=1), chips, split_axis=0, concat_axis=0, tiled=True
+    )
+    grad_heads = grad_got[:, :DH]
+    vector_sums = jnp.sum(grad_got[:, DH : DH + 2].astype(f32), axis=(0, 1))
+    final_vectors = vector_sums[: 4 * share].reshape(4, share)
+    final_fc_b = vector_sums[4 * share : 4 * share + hidden_share]
+
+    final_proj_w = lax.psum_scatter(grad_proj_w, chips, scatter_dimension=0, tiled=True).astype(f32)
+    fc_terms = grad_fc_w.reshape(zx, 2, 2, share, hidden_half).transpose(0, 2, 1, 3, 4).reshape(width, hidden_half)
+    fc_sum = lax.psum_scatter(fc_terms, chips, scatter_dimension=0, tiled=True).reshape(2, share, hidden_half)
+    final_out_w = lax.psum_scatter(grad_out_w, chips, scatter_dimension=0, tiled=True).astype(f32)
+    fc_keep = lax.dynamic_index_in_dim(fc_sum, ic, 0, keepdims=False)
+    fc_give = swap(lax.dynamic_index_in_dim(fc_sum, 1 - ic, 0, keepdims=False), "core")
+    final_fc_w = in_order(
+        fc_keep.reshape(share, zx, 2, hidden_share), fc_give.reshape(share, zx, 2, hidden_share), ic, 2
+    )
+    final_fc_w = final_fc_w.reshape(share, 2 * hidden_half).astype(f32)
+
+    slot_grads, send_grads = attend_backward(
+        bound, inloc, outloc, grad_heads, queries, keys, values, attn_t, lse
+    )
+    grads_got = lax.all_to_all(send_grads, chips, split_axis=0, concat_axis=0, tiled=True)
+
+    count = 0
+    raw_term = jnp.zeros((width, 3 * DH), f32)
+    for piece in pieces:
+        raw_term = raw_term + product_tn(piece, slot_grads[count : count + piece.shape[0]])
+        count += piece.shape[0]
+    column_sums = jnp.sum(slot_grads.astype(f32), axis=0)
+    high, low = split_float(column_sums)
+    tail = jnp.concatenate([high[None], low[None], jnp.zeros((6, 3 * DH), bf16)], axis=0)
+    raw_send = jnp.concatenate(
+        [
+            raw_term.astype(bf16).reshape(devices, share, 3 * DH),
+            jnp.broadcast_to(tail[None], (devices, 8, 3 * DH)),
+        ],
+        axis=1,
+    )
+    raw_got = lax.all_to_all(raw_send, every, split_axis=0, concat_axis=0, tiled=True)
+    raw_sum = jnp.sum(raw_got.reshape(heads, 2, share + 8, 3 * DH).astype(f32), axis=1)
+    raw_grad = raw_sum[:, :share].reshape(heads, share, 3, DH).transpose(1, 2, 0, 3).reshape(share, 3 * width)
+    all_sums = (raw_sum[:, share] + raw_sum[:, share + 1]).reshape(heads, 3, DH).transpose(1, 0, 2)
+    all_sums = all_sums.reshape(3 * width)
+    final_qkv_w = raw_grad * gain_one[:, None] + shift_one[:, None] * all_sums[None, :]
+    final_gain_one = jnp.sum(raw_grad * raw_qkv, axis=1)
+    final_shift_one = jnp.sum(raw_qkv * all_sums[None, :], axis=1)
+    final_q_b = lax.dynamic_slice(all_sums, (place,), (share,))
+    final_v_b = lax.dynamic_slice(all_sums, (2 * width + place,), (share,))
+
+    grads_in = grads_got.reshape(zx, 2, 3 * DH, 2, rows).transpose(0, 2, 3, 1, 4).reshape(3 * local, 2 * own)
+    back = lax.dot_general(grads_in, w_qkv, (((0,), (1,)), ((), ())), preferred_element_type=f32)
+    back_own = back[:own] + swap(back[own:].astype(bf16), "core").astype(f32)
+    back_own = back_own.reshape(micro, rows, width)
+    input_grad = grad_resid[:own].reshape(micro, rows, width) + norm_back(back_own, normed_one, inverse_one)
+
+    return (
+        output.reshape(micro, rows, width),
+        input_grad.astype(bf16),
+        final_qkv_w,
+        final_q_b,
+        final_v_b,
+        final_out_w,
+        final_vectors[2],
+        final_gain_one,
+        final_shift_one,
+        final_vectors[0],
+        final_vectors[1],
+        final_fc_w,
+        final_fc_b,
+        final_proj_w,
+        final_vectors[3],
+    )
+
+
+def specs(names):
+    rows, vector, tokens = P(names, None), P(names), P(None, names, None)
+    weights = (rows, vector, vector, rows, vector, vector, vector, vector, vector, rows, vector, rows, vector)
+    return (tokens, *weights, tokens, P(), P()), (tokens, tokens, *weights)
+
+
 def solution(mesh):
-    in_specs = (
-        P(None, ("blk", "head"), None),
-        P(("blk", "head"), None),
-        P(("blk", "head")),
-        P(("blk", "head")),
-        P(("blk", "head"), None),
-        P(("blk", "head")),
-        P(("blk", "head")),
-        P(("blk", "head")),
-        P(("blk", "head")),
-        P(("blk", "head")),
-        P(("blk", "head"), None),
-        P(("blk", "head")),
-        P(("blk", "head"), None),
-        P(("blk", "head")),
-        P(None, ("blk", "head"), None),
-        P(),
-        P(),
-    )
-    out_specs = (
-        P(None, ("blk", "head"), None),
-        P(None, ("blk", "head"), None),
-        P(("blk", "head"), None),
-        P(("blk", "head")),
-        P(("blk", "head")),
-        P(("blk", "head"), None),
-        P(("blk", "head")),
-        P(("blk", "head")),
-        P(("blk", "head")),
-        P(("blk", "head")),
-        P(("blk", "head")),
-        P(("blk", "head"), None),
-        P(("blk", "head")),
-        P(("blk", "head"), None),
-        P(("blk", "head")),
-    )
-    return jax.shard_map(body, mesh=mesh, in_specs=in_specs, out_specs=out_specs, check_vma=False)
+    sizes = dict(mesh.shape)
+    if sizes["head"] == 2 and sizes["blk"] == 16:
+        fine = Mesh(mesh.devices.reshape(2, 4, 2, 2), ("head", "z", "x", "core"))
+        given, made = specs(("z", "x", "core", "head"))
+        return jax.shard_map(fast_body, mesh=fine, in_specs=given, out_specs=made, check_vma=False)
+    given, made = specs(("blk", "head"))
+    return jax.shard_map(general_body, mesh=mesh, in_specs=given, out_specs=made, check_vma=False)

time: 2480 us -> 631 us (0.25)
  blocking collectives: 871 us -> 0 us
  waiting for transfers between devices: 1080 us -> 314 us
  matrix products: 200 us -> 53.8 us
  local copies, waits for them, and re-layouts: 188 us -> 76.3 us
  Pallas kernels: 0 us -> 55.9 us
  starting transfers between devices: 22.7 us -> 68 us
  other arithmetic: 78.6 us -> 35.1 us
    unnamed x3 -> x0, blocking collectives: 788 us -> none
    reduce_scatter x4 -> x3, waiting for transfers between devices: 777 us -> 139 us  [the longest x1 93.8 us: fast_body(): lax.psum_scatter(grad_proj_w, chips, scatter_dimension=0, tiled=True)]
    all_gather x8 -> x2, waiting for transfers between devices: 279 us -> 0.02 us  [the longest x1 0.02 us: fast_body(): w_qkv = lax.all_gather(packed_qkv, chips, axis=0)]
    ppermute x0 -> x27, waiting for transfers between devices: none -> 131 us  [the longest x6 88.3 us: shifted(): lax.ppermute(values, 'z', [(i, (i + step) % count) for i in range(count)])]
    dynamic_update_slice x16 -> x0, local copies, waits for them, and re-layouts: 103 us -> none  [one_step(): buffer = lax.dynamic_update_slice(buffer, term, (offset, 0, 0))]
    dot_general x56 -> x1, matrix products: 104 us -> 1.84 us  [fast_body(): lax.dot_general(grads_in, w_qkv, (((0,), (1,)), ((), ())), preferred_elem...]
    pallas_call x0 -> x2, Pallas kernels: none -> 55.9 us  [the longest x1 30.6 us: attend_backward(): pl.pallas_call(functools.partial(backward_kernel, head_size), out_shape=(...]
    all_gather x1 -> x0, blocking collectives: 50.4 us -> none  [body(): lax.all_gather(shards[10], ('blk', 'head'), axis=0, tiled=True)]
  transfers between devices with their start and end apart: 18 -> 37, of which waited for: 14 -> 13; matrix products, arithmetic and copies ran while one was open for 17% -> 24% of each run, Pallas kernels for 0% -> 9%
where the time goes in v1:
time: 631 us; the launch traced here: 619 us
  waiting for transfers between devices  314 us (50%)
  local copies, waits for them, and re-layouts  76.3 us (12%)
  starting transfers between devices  68 us (11%)
  Pallas kernels  55.9 us (9%)
  matrix products  53.8 us (9%)
  other arithmetic  35.1 us (6%)
  between operations  15.7 us (2%)
    reduce_scatter x1, waiting for transfers between devices, fast_body(): lax.psum_scatter(grad_proj_w, chips, scatter_dimension=0, tiled=True)  93.8 us
    ppermute x6, waiting for transfers between devices, shifted(): lax.ppermute(values, 'z', [(i, (i + step) % count) for i in range(count)])  88.3 us
    reduce_scatter x1, waiting for transfers between devices, fast_body(): lax.psum_scatter(fc_terms, chips, scatter_dimension=0, tiled=True)  45.5 us
    ppermute x21, waiting for transfers between devices, swap(): return lax.ppermute(values, axis, PAIR)  43 us
    all_to_all x1, waiting for transfers between devices, fast_body(): lax.all_to_all(send_grads, chips, split_axis=0, concat_axis=0, tiled=True)  31.5 us
    pallas_call x1, Pallas kernels, attend_backward(): pl.pallas_call(functools.partial(backward_kernel, head_size), out_shape=(...  30.6 us
    pallas_call x1, Pallas kernels, attend_forward(): pl.pallas_call(functools.partial(forward_kernel, head_size), out_shape=(j...  25.2 us
    dot_general x15, matrix products, product_tn(): lax.dot_general(left, right, (((0,), (0,)), ((), ())), preferred_element_...  21.1 us
  transfers between devices with their start and end apart: 37, of which 13 were waited for; matrix products, arithmetic and copies ran while one was open for 24% of the time, Pallas kernels for 9%

profile of v1, /device:TPU:11, one launch (start us, length us, event | category | flops | bytes accessed | tf_op | source)
XLA Modules:
  0.0 619.1 jit_solution(11004261606424097565)
XLA Ops:
  23.2 5.3 all-to-all-start
  32.0 8.7 %collective-permute-done.2 = bf16[128,1024]{1,0:T(8,128)(2,1)S(1)} collective-permute-done((bf16[128,1024]{1,0:T(8,128)(2,1)S(1)}, bf16[128,1024]{1,0:T(8,128)(2,1)S(1)}, u32[]{:S(2)}, u32[]{:S(2)}) %collective-permute-start.2) | collective-permute-done | bytes 262176 | tf_op jit(solution)/shard_map/ppermute | solution.py:685
  40.7 18.5 %collective-permute-done.1 = bf16[128,1024]{1,0:T(8,128)(2,1)S(1)} collective-permute-done((bf16[128,1024]{1,0:T(8,128)(2,1)S(1)}, bf16[128,1024]{1,0:T(8,128)(2,1)S(1)}, u32[]{:S(2)}, u32[]{:S(2)}) %collective-permute-start.1) | collective-permute-done | bytes 262176 | tf_op jit(solution)/shard_map/ppermute | solution.py:685
  66.6 39.8 %collective-permute-done.6 = bf16[128,1024]{1,0:T(8,128)(2,1)} collective-permute-done((bf16[128,1024]{1,0:T(8,128)(2,1)}, bf16[128,1024]{1,0:T(8,128)(2,1)}, u32[]{:S(2)}, u32[]{:S(2)}) %collective-permute-start.6) | collective-permute-done | bytes 262176 | tf_op jit(solution)/shard_map/ppermute | solution.py:674
  107.6 4.0 collective-permute-start.8
  116.0 61.2 %collective-permute-done.7 = bf16[2,128,1024]{2,1,0:T(8,128)(2,1)} collective-permute-done((bf16[2,128,1024]{2,1,0:T(8,128)(2,1)S(1)}, bf16[2,128,1024]{2,1,0:T(8,128)(2,1)}, u32[]{:S(2)}, u32[]{:S(2)}) %collective-permute-start.7) | collective-permute-done | bytes 524320 | tf_op jit(solution)/shard_map/ppermute | solution.py:685
  187.3 25.2 %attend_forward.1 = (bf16[16,64,256]{2,1,0:T(8,128)(2,1)}, bf16[4096,64]{1,0:T(8,128)(2,1)S(1)}, bf16[4096,64]{1,0:T(8,128)(2,1)S(1)}, bf16[4096,64]{1,0:T(8,128...) custom-call(s32[1]{0:T(128)S(1)} %bitcast.207, s32[64]{0:T(128)S(1)} %get-tuple-element.40.inloc, ...), custom_call_target="tpu_custom_call" | custom-call | flops 8589934592 | bytes 8388608 | tf_op jit(solution)/shard_map/attend_forward/pallas_call | solution.py:544
  213.4 20.9 %all-to-all-start.1 = ((bf16[16,64,256]{2,1,0:T(8,128)(2,1)}), bf16[16,64,256]{2,1,0:T(8,128)(2,1)}, u32[]{:S(2)}, u32[]{:S(2)}) async-start(bf16[16,64,256]{2,1,0:T(8,128)(2,1)} %get-tuple-element.24), calls=%async_computation.1 | async-start | bytes 1048576 | tf_op jit(solution)/shard_map/all_to_all | solution.py:852
  242.7 5.4 all-to-all-done.1
  264.1 6.3 %fusion.105 = (bf16[16,128,1024]{2,1,0:T(8,128)(2,1)}, bf16[16,128,1024]{2,1,0:T(8,128)(2,1)}) fusion(bf16[16,296,1024]{2,1,0:T(8,128)(2,1)} %bitcast.215), kind=kLoop, calls=%fused_computation.240 | loop fusion | bytes 16777216 | tf_op jit(solution)/shard_map/slice | solution.py:825
  270.4 8.6 %copy.315 = bf16[8,2,2,32,2,1024]{5,4,3,2,1,0:T(2,128)(2,1)} copy(bf16[8,2,2,32,2,1024]{5,3,1,4,2,0:T(8,128)(2,1)} %bitcast.212) | data formatting | bytes 8388608 | tf_op jit(solution)/shard_map/transpose | solution.py:826
  279.0 3.7 copy.344
  287.8 5.9 convert_reduce_fusion.1
  304.7 4.8 convolution_convert_fusion.1
  326.4 4.8 all-to-all-start.2
  331.4 6.4 %fusion.98 = f32[512,1024]{1,0:T(8,128)S(1)} fusion(bf16[2048,1024]{1,0:T(8,128)(2,1)} %bitcast.227, f32[512,2048]{1,0:T(8,128)} %copy-done.55, f32[2048]{0:T(1024)S(1)} %fusion.84), kind=kOutput, calls=%fused_computation.236 | convolution fusion | flops 2157969408 | bytes 10493952 | tf_op jit(solution)/shard_map/dot_general | solution.py:35
  341.0 5.3 convolution_convert_fusion
  350.4 30.6 %attend_backward.1 = (bf16[4096,192]{1,0:T(8,128)(2,1)}, bf16[16,192,256]{2,1,0:T(8,128)(2,1)}) custom-call(s32[1]{0:T(128)S(1)} %bitcast.208, s32[64]{0:T(128)S(1)} %get-tuple-element.40.inloc, s32[64]{0:T(128)S(1)} %get-tuple-element.39.outloc, bf16[16,64,256]{2,1,0:T(8,128)(2,1)S(1)} %slice.224.grad_t, bf16[4096,64]{1,0:T(8,128)(2,1)S(1)} %get-tuple-element.25.qs, ...), custom_call_target="tpu_custom_call" | custom-call | flops 21474836480 | bytes 16777216 | tf_op jit(solution)/shard_map/attend_backward/pallas_call | solution.py:647
  381.0 5.3 all-to-all-start.3
  398.4 31.5 %all-to-all-done.3 = bf16[16,192,256]{2,1,0:T(8,128)(2,1)} async-done(((bf16[16,192,256]{2,1,0:T(8,128)(2,1)}), bf16[16,192,256]{2,1,0:T(8,128)(2,1)}, u32[]{:S(2)}, u32[]{:S(2)}) %all-to-all-start.3) | async-done | bytes 1572896 | tf_op jit(solution)/shard_map/all_to_all | solution.py:914
  429.9 5.5 all-to-all-start.4
  453.2 4.8 all-to-all-done.4
  466.1 45.5 %reduce-scatter.6.cloned.1.call-done = bf16[64,2048]{1,0:T(8,128)(2,1)} async-done(((bf16[1024,2048]{1,0:T(8,128)(2,1)}), bf16[64,2048]{1,0:T(8,128)(2,1)}) %reduce-scatter.6.cloned.1.call-update) | async-done | bytes 262160 | tf_op jit(solution)/shard_map/reduce_scatter | solution.py:902
  514.7 93.8 %reduce-scatter.8.cloned.1.call-done = bf16[128,1024]{1,0:T(8,128)(2,1)} async-done(((bf16[2048,1024]{1,0:T(8,128)(2,1)}), bf16[128,1024]{1,0:T(8,128)(2,1)}) %reduce-scatter.8.cloned.1.call-update) | async-done | bytes 262160 | tf_op jit(solution)/shard_map/reduce_scatter | solution.py:900
  (365 shorter events, 151.6 us)
Async XLA Ops:
  7.2 247.5 %all-gather.5.cloned.1.call-start = ((), (), s32[]{:S(2)}) async-start(), calls=%async_computation.11 | async-start | bytes 10305536 | tf_op jit(solution)/shard_map/all_gather | solution.py:819
  14.8 25.8 %collective-permute-start.2 = (bf16[128,1024]{1,0:T(8,128)(2,1)S(1)}, bf16[128,1024]{1,0:T(8,128)(2,1)S(1)}, u32[]{:S(2)}, u32[]{:S(2)}) collective-permute-start(bf16[128,1024]{1,0:T(8,128)(2,1)S(1)} %bitcast.250), channel_id=1, source_target_pairs={{0,8},{4,12},{8,0},{12,4},{1,9},{5,13},{9,1},{13,5},{2,10},{6,14},... | collective-permute-start | bytes 786440 | tf_op jit(solution)/shard_map/ppermute | solution.py:685
  17.1 42.0 %collective-permute-start.1 = (bf16[128,1024]{1,0:T(8,128)(2,1)S(1)}, bf16[128,1024]{1,0:T(8,128)(2,1)S(1)}, u32[]{:S(2)}, u32[]{:S(2)}) collective-permute-start(bf16[128,1024]{1,0:T(8,128)(2,1)S(1)} %bitcast.251), channel_id=1, source_target_pairs={{0,4},{4,8},{8,12},{12,0},{1,5},{5,9},{9,13},{13,1},{2,6},{6,10},{... | collective-permute-start | bytes 786440 | tf_op jit(solution)/shard_map/ppermute | solution.py:685
  23.2 88.6 %all-to-all-start = ((bf16[32,40,192]{2,1,0:T(8,128)(2,1)}), bf16[32,40,192]{2,1,0:T(8,128)(2,1)S(1)}, u32[]{:S(2)}, u32[]{:S(2)}) async-start(bf16[32,40,192]{2,1,0:T(8,128)(2,1)} %bitcast.43), calls=%async_computation | async-start | bytes 1310720 | tf_op jit(solution)/shard_map/all_to_all | solution.py:757
  28.5 31.1 %collective-permute-start.5 = (bf16[128,1024]{1,0:T(8,128)(2,1)}, bf16[128,1024]{1,0:T(8,128)(2,1)}, u32[]{:S(2)}, u32[]{:S(2)}) collective-permute-start(bf16[128,1024]{1,0:T(8,128)(2,1)} %get-tuple-element.57), channel_id=1, source_target_pairs={{0,16},{16,0},{1,17},{17,1},{2,18},{18,2},{3,19},{19,3},{4,20},{20... | collective-permute-start | bytes 786440 | tf_op jit(solution)/shard_map/ppermute | solution.py:674
  59.3 53.1 %collective-permute-start.4 = (bf16[4,128,1024]{2,1,0:T(8,128)(2,1)S(1)}, bf16[4,128,1024]{2,1,0:T(8,128)(2,1)S(1)}, u32[]{:S(2)}, u32[]{:S(2)}) collective-permute-start(bf16[4,128,1024]{2,1,0:T(8,128)(2,1)S(1)} %pad_maximum_fusion.1), channel_id=1, source_target_pairs={{0,2},{2,0},{1,3},{3,1},{4,6},{6,4},{5,7},{7,5},{8,10},{10,8},{9,1... | collective-permute-start | bytes 3145736 | tf_op jit(solution)/shard_map/ppermute | solution.py:674
  59.6 46.7 %collective-permute-start.6 = (bf16[128,1024]{1,0:T(8,128)(2,1)}, bf16[128,1024]{1,0:T(8,128)(2,1)}, u32[]{:S(2)}, u32[]{:S(2)}) collective-permute-start(bf16[128,1024]{1,0:T(8,128)(2,1)} %collective-permute-done.5), channel_id=1, source_target_pairs={{0,2},{2,0},{1,3},{3,1},{4,6},{6,4},{5,7},{7,5},{8,10},{10,8},{9,1... | collective-permute-start | bytes 786440 | tf_op jit(solution)/shard_map/ppermute | solution.py:674
  63.8 118.5 %collective-permute-start.10 = (bf16[4,128,1024]{2,1,0:T(8,128)(2,1)S(1)}, bf16[4,128,1024]{2,1,0:T(8,128)(2,1)}, u32[]{:S(2)}, u32[]{:S(2)}) collective-permute-start(bf16[4,128,1024]{2,1,0:T(8,128)(2,1)S(1)} %pad_maximum_fusion.1), channel_id=1, source_target_pairs={{0,1},{1,0},{2,3},{3,2},{4,5},{5,4},{6,7},{7,6},{8,9},{9,8},{10,11... | collective-permute-start | bytes 3145736 | tf_op jit(solution)/shard_map/ppermute | solution.py:674
  107.5 71.4 %collective-permute-start.9 = (bf16[2,128,1024]{2,1,0:T(8,128)(2,1)S(1)}, bf16[2,128,1024]{2,1,0:T(8,128)(2,1)}, u32[]{:S(2)}, u32[]{:S(2)}) collective-permute-start(bf16[2,128,1024]{2,1,0:T(8,128)(2,1)S(1)} %pad_maximum_fusion.6), channel_id=1, source_target_pairs={{0,12},{4,0},{8,4},{12,8},{1,13},{5,1},{9,5},{13,9},{2,14},{6,2},{... | collective-permute-start | bytes 1572872 | tf_op jit(solution)/shard_map/ppermute | solution.py:685
  107.6 71.6 %collective-permute-start.8 = (bf16[2,128,1024]{2,1,0:T(8,128)(2,1)S(1)}, bf16[2,128,1024]{2,1,0:T(8,128)(2,1)}, u32[]{:S(2)}, u32[]{:S(2)}) collective-permute-start(bf16[2,128,1024]{2,1,0:T(8,128)(2,1)S(1)} %pad_maximum_fusion.6), channel_id=1, source_target_pairs={{0,8},{4,12},{8,0},{12,4},{1,9},{5,13},{9,1},{13,5},{2,10},{6,14},... | collective-permute-start | bytes 1572872 | tf_op jit(solution)/shard_map/ppermute | solution.py:685
  111.6 65.6 %collective-permute-start.7 = (bf16[2,128,1024]{2,1,0:T(8,128)(2,1)S(1)}, bf16[2,128,1024]{2,1,0:T(8,128)(2,1)}, u32[]{:S(2)}, u32[]{:S(2)}) collective-permute-start(bf16[2,128,1024]{2,1,0:T(8,128)(2,1)S(1)} %pad_maximum_fusion.6), channel_id=1, source_target_pairs={{0,4},{4,8},{8,12},{12,0},{1,5},{5,9},{9,13},{13,1},{2,6},{6,10},{... | collective-permute-start | bytes 1572872 | tf_op jit(solution)/shard_map/ppermute | solution.py:685
  112.8 71.2 %collective-permute-start.11 = (bf16[4,128,1024]{2,1,0:T(8,128)(2,1)S(1)}, bf16[4,128,1024]{2,1,0:T(8,128)(2,1)S(1)}, u32[]{:S(2)}, u32[]{:S(2)}) collective-permute-start(bf16[4,128,1024]{2,1,0:T(8,128)(2,1)S(1)} %collective-permute-done.4), channel_id=1, source_target_pairs={{0,1},{1,0},{2,3},{3,2},{4,5},{5,4},{6,7},{7,6},{8,9},{9,8},{10,11... | collective-permute-start | bytes 3145736 | tf_op jit(solution)/shard_map/ppermute | solution.py:674
  177.2 59.4 %collective-permute-start.24 = (bf16[32,1536]{1,0:T(8,128)(2,1)}, bf16[32,1536]{1,0:T(8,128)(2,1)}, u32[]{:S(2)}, u32[]{:S(2)}) collective-permute-start(bf16[32,1536]{1,0:T(8,128)(2,1)} %reshape.647), channel_id=1, source_target_pairs={{0,1},{1,0},{2,3},{3,2},{4,5},{5,4},{6,7},{7,6},{8,9},{9,8},{10,11... | collective-permute-start | bytes 294920 | tf_op jit(solution)/shard_map/ppermute | solution.py:674
  213.4 34.8 %all-to-all-start.1 = ((bf16[16,64,256]{2,1,0:T(8,128)(2,1)}), bf16[16,64,256]{2,1,0:T(8,128)(2,1)}, u32[]{:S(2)}, u32[]{:S(2)}) async-start(bf16[16,64,256]{2,1,0:T(8,128)(2,1)} %get-tuple-element.24), calls=%async_computation.1 | async-start | bytes 1048576 | tf_op jit(solution)/shard_map/all_to_all | solution.py:852
  234.3 212.3 %all-gather.7.cloned.1.call-start = ((), (), s32[]{:S(2)}) async-start(), calls=%async_computation.12 | async-start | bytes 3342336 | tf_op jit(solution)/shard_map/all_gather | solution.py:840
  258.7 204.1 %reduce-scatter.4.cloned.1.call-start = ((), (), s32[]{:S(2)}) async-start(), calls=%async_computation.8 | async-start | bytes 1114112 | tf_op jit(solution)/shard_map/reduce_scatter | solution.py:903
  262.3 20.4 %collective-permute-start.18 = (bf16[256,1024]{1,0:T(8,128)(2,1)}, bf16[256,1024]{1,0:T(8,128)(2,1)}, u32[]{:S(2)}, u32[]{:S(2)}) collective-permute-start(bf16[256,1024]{1,0:T(8,128)(2,1)} %get-tuple-element.55), channel_id=1, source_target_pairs={{0,1},{1,0},{2,3},{3,2},{4,5},{5,4},{6,7},{7,6},{8,9},{9,8},{10,11... | collective-permute-start | bytes 1572872 | tf_op jit(solution)/shard_map/ppermute | solution.py:674
  304.6 207.0 %reduce-scatter.6.cloned.1.call-start = ((), (), s32[]{:S(2)}) async-start(), calls=%async_computation.9 | async-start | bytes 4456448 | tf_op jit(solution)/shard_map/reduce_scatter | solution.py:902
  326.4 21.9 %all-to-all-start.2 = ((bf16[16,72,256]{2,1,0:T(8,128)(2,1)}), bf16[16,72,256]{2,1,0:T(8,128)(2,1)}, u32[]{:S(2)}, u32[]{:S(2)}) async-start(bf16[16,72,256]{2,1,0:T(8,128)(2,1)} %pad_maximum_fusion.5), calls=%async_computation.2 | async-start | bytes 1179648 | tf_op jit(solution)/shard_map/all_to_all | solution.py:892
  331.1 277.4 %reduce-scatter.8.cloned.1.call-start = ((), (), s32[]{:S(2)}) async-start(), calls=%async_computation.10 | async-start | bytes 4456448 | tf_op jit(solution)/shard_map/reduce_scatter | solution.py:900
  340.0 95.4 %collective-permute-start.20 = (bf16[256,1024]{1,0:T(8,128)(2,1)}, bf16[256,1024]{1,0:T(8,128)(2,1)}, u32[]{:S(2)}, u32[]{:S(2)}) collective-permute-start(bf16[256,1024]{1,0:T(8,128)(2,1)} %slice.277), channel_id=1, source_target_pairs={{0,1},{1,0},{2,3},{3,2},{4,5},{5,4},{6,7},{7,6},{8,9},{9,8},{10,11... | collective-permute-start | bytes 1572872 | tf_op jit(solution)/shard_map/ppermute | solution.py:674
  381.0 48.9 %all-to-all-start.3 = ((bf16[16,192,256]{2,1,0:T(8,128)(2,1)}), bf16[16,192,256]{2,1,0:T(8,128)(2,1)}, u32[]{:S(2)}, u32[]{:S(2)}) async-start(bf16[16,192,256]{2,1,0:T(8,128)(2,1)} %get-tuple-element.30), calls=%async_computation.3 | async-start | bytes 3145728 | tf_op jit(solution)/shard_map/all_to_all | solution.py:914
  429.9 28.1 %all-to-all-start.4 = ((bf16[32,40,192]{2,1,0:T(8,128)(2,1)}), bf16[32,40,192]{2,1,0:T(8,128)(2,1)}, u32[]{:S(2)}, u32[]{:S(2)}) async-start(bf16[32,40,192]{2,1,0:T(8,128)(2,1)} %pad_maximum_fusion.3), calls=%async_computation.4 | async-start | bytes 1310720 | tf_op jit(solution)/shard_map/all_to_all | solution.py:931
  512.6 97.7 %collective-permute-start.26 = (bf16[32,2048]{1,0:T(8,128)(2,1)S(1)}, bf16[32,2048]{1,0:T(8,128)(2,1)S(1)}, u32[]{:S(2)}, u32[]{:S(2)}) collective-permute-start(bf16[32,2048]{1,0:T(8,128)(2,1)S(1)} %get-tuple-element.65), channel_id=1, source_target_pairs={{0,1},{1,0},{2,3},{3,2},{4,5},{5,4},{6,7},{7,6},{8,9},{9,8},{10,11... | collective-permute-start | bytes 393224 | tf_op jit(solution)/shard_map/ppermute | solution.py:674
  (71 other events, 774.1 us)
Sparse Core Ops, SparseCore 0:
  13.3 195.0 all-gather.4
  258.8 67.0 all-gather.6
  328.2 57.2 reduce-scatter.3
  387.7 123.8 reduce-scatter.5
  513.9 94.6 reduce-scatter.7

commit v2 on v1

--- a/solution.py
+++ b/solution.py
@@ -667,23 +667,407 @@
     )(bound, inloc, outloc, grad_t, qs, ks, vs, attn_t, lse)
 
 
+HALF_STEP = 512
+
+
+def gelu_pair(values):
+    cubic = values * values
+    inner = 0.7978845608028654 * values * (1.0 + 0.044715 * cubic)
+    bent = jnp.tanh(inner)
+    slope = 0.7978845608028654 * (1.0 + 0.134145 * cubic)
+    half = 0.5 * (1.0 + bent)
+    return values * half, half + 0.5 * values * (1.0 - bent * bent) * slope
+
+
+def load_rows(table, pieces, targets, sem, wait):
+    slot = 0
+    for piece in pieces:
+        count = piece.shape[0]
+
+        @pl.loop(0, count)
+        def _(index, piece=piece, slot=slot):
+            chip = table[0, slot + index]
+            for rows, target in targets(chip):
+                copy = pltpu.make_async_copy(piece.at[index, rows], target, sem)
+                if wait:
+                    copy.wait()
+                else:
+                    copy.start()
+
+        slot += count
+
+
+def project_kernel(count, table, got, *refs):
+    pieces, (part_out, sent, attn_in, w_out, sem) = refs[:count], refs[count:]
+    chips, size, span = got.shape
+    share = w_out.shape[0] // chips
+    rows = span // 2
+
+    def targets(chip):
+        return [(pl.ds(0, share), w_out.at[rows_at(chip, share)])]
+
+    load_rows(table, pieces, targets, sem, False)
+    for chip in range(chips):
+        micro, head = divmod(chip, chips // 2)
+        for rel in range(2):
+            column = (rel * 2 + micro) * rows
+            attn_in[head * size : (head + 1) * size, column : column + rows] = got[chip, :, rel * rows : (rel + 1) * rows]
+    load_rows(table, pieces, targets, sem, True)
+    left = attn_in[...].astype(jnp.float32).T.astype(jnp.bfloat16)
+    part = dot_nn(left, w_out[...])
+    part_out[...] = part
+    sent[...] = part.astype(jnp.bfloat16)
+
+
+def project(table, got, pieces, share):
+    chips, size, span = got.shape
+    width = pieces[0].shape[2]
+    tokens = 2 * span
+    bf16 = jnp.bfloat16
+    return pl.pallas_call(
+        functools.partial(project_kernel, len(pieces)),
+        out_shape=(
+            jax.ShapeDtypeStruct((tokens, width), jnp.float32),
+            jax.ShapeDtypeStruct((tokens, width), bf16),
+            jax.ShapeDtypeStruct((chips // 2 * size, tokens), bf16),
+        ),
+        in_specs=[pl.BlockSpec(memory_space=SM), pl.BlockSpec(memory_space=VM)]
+        + [pl.BlockSpec(memory_space=pl.ANY)] * len(pieces),
+        out_specs=[pl.BlockSpec(memory_space=VM)] * 3,
+        scratch_shapes=[VM((chips * share, width), bf16), pltpu.SemaphoreType.DMA],
+        compiler_params=pltpu.CompilerParams(vmem_limit_bytes=24 * 1024 * 1024),
+        cost_estimate=pl.CostEstimate(
+            flops=2 * tokens * chips * share * width, bytes_accessed=8 * tokens * width, transcendentals=0
+        ),
+        name="project",
+    )(table, got, *pieces)
+
+
+def middle_kernel(count, share, table, x_a, x_b, g_a, g_b, part, got_a, got_b, vectors, fc_bias, *refs):
+    pieces = refs[:count]
+    (resid, base, other, grad_act, grad_sent, fc_sums, terms) = refs[count : count + 7]
+    (w_fc, w_proj, g_all, act, act_t, rest, proj_buf, fc_buf, load_sem, proj_sem, fc_sem) = refs[count + 7 :]
+    f32, bf16 = jnp.float32, jnp.bfloat16
+    tokens, width = part.shape
+    own = tokens // 2
+    hidden = w_proj.shape[0]
+    chips = terms.shape[0]
+    each = hidden // chips
+    folds = hidden // width
+    fc_row = share + each
+
+    def targets(chip):
+        wanted = [(pl.ds(share, each), w_proj.at[rows_at(chip, each)])]
+        for fold in range(folds):
+            for core in range(2):
+                first = fc_row + (fold * 2 + core) * share
+                place = ((chip // 2) * 2 + core) * 2 + chip % 2
+                wanted.append(
+                    (pl.ds(first, share), w_fc.at[rows_at(place, share), pl.ds(fold * width, width)])
+                )
+        return wanted
+
+    load_rows(table, pieces, targets, load_sem, False)
+    for half, (x_in, g_in, arrived) in enumerate(((x_a, g_a, got_a), (x_b, g_b, got_b))):
+        here = slice(half * own, (half + 1) * own)
+        g_all[here, :] = g_in[...]
+        value = x_in[...].astype(f32) + part[here, :] + arrived[...].astype(f32) + vectors[2:3, :]
+        resid[here, :] = value
+        centred = value - jnp.mean(value, axis=-1, keepdims=True)
+        inverse = lax.rsqrt(jnp.mean(centred * centred, axis=-1, keepdims=True) + 1e-05)
+        rounded = (centred * inverse * vectors[0:1, :] + vectors[1:2, :]).astype(bf16)
+        act[here, :] = rounded
+        act_t[:, here] = rounded.astype(f32).T.astype(bf16)
+    base[...] = resid[:own, :] + vectors[3:4, :]
+    load_rows(table, pieces, targets, load_sem, True)
+
+    per_step = HALF_STEP // each
+
+    def copies(step, slot):
+        made = []
+        for index in range(per_step):
+            made.append(
+                pltpu.make_async_copy(
+                    proj_buf.at[slot, pl.ds(index * each, each)],
+                    terms.at[table[1, step * per_step + index], pl.ds(0, each)],
+                    proj_sem.at[slot],
+                )
+            )
+        fold = step // (width // HALF_STEP)
+        column = pl.multiple_of(step % (width // HALF_STEP) * HALF_STEP, HALF_STEP)
+        for chip in range(chips):
+            for core in range(2):
+                place = ((chip // 2) * 2 + core) * 2 + chip % 2
+                made.append(
+                    pltpu.make_async_copy(
+                        fc_buf.at[slot, pl.ds(place * share, share)],
+                        terms.at[
+                            table[1, chip],
+                            pl.ds(pl.multiple_of(each + share + (fold * 2 + core) * share, 16), share),
+                            pl.ds(column, HALF_STEP),
+                        ],
+                        fc_sem.at[slot],
+                    )
+                )
+        return made
+
+    steps = hidden // HALF_STEP
+
+    @pl.loop(0, steps)
+    def _(step):
+        slot = step % 2
+        columns = pl.ds(pl.multiple_of(step * HALF_STEP, HALF_STEP), HALF_STEP)
+        rows = rows_at(step, HALF_STEP)
+
+        @pl.when(step >= 2)
+        def _():
+            for copy in copies(step - 2, slot):
+                copy.wait()
+
+        grads = g_all[...]
+        value, slope = gelu_pair(dot_nn(act[...], w_fc[:, columns]) + fc_bias[:, columns])
+        value = value.astype(bf16)
+        proj_buf[slot] = dot_nn(value.astype(f32).T.astype(bf16), grads).astype(bf16)
+        grad_pre = (dot_nt(grads, w_proj[rows, :]) * slope).astype(bf16)
+        fc_sums[:, columns] = jnp.sum(grad_pre.astype(f32), axis=0, keepdims=True)
+        fc_buf[slot] = dot_nn(act_t[...], grad_pre).astype(bf16)
+        for copy in copies(step, slot):
+            copy.start()
+        projected = dot_nn(value, w_proj[rows, :])
+        back = dot_nt(grad_pre, w_fc[:, columns])
+        base[...] += projected[:own]
+
+        @pl.when(step == 0)
+        def _():
+            grad_act[...] = back
+            rest[...] = projected[own:]
+
+        @pl.when(step > 0)
+        def _():
+            grad_act[...] += back
+            rest[...] += projected[own:]
+
+    other[...] = rest[...].astype(bf16)
+    grad_sent[...] = grad_act[...].astype(bf16)
+    for step in range(steps - 2, steps):
+        for copy in copies(step, step % 2):
+            copy.wait()
+
+
+def middle(table, x_a, x_b, g_a, g_b, part, got_a, got_b, vectors, fc_bias, pieces, share):
+    tokens, width = part.shape
+    f32, bf16 = jnp.float32, jnp.bfloat16
+    hidden = fc_bias.shape[1]
+    chips = table.shape[1]
+    each = hidden // chips
+    rows = share + each + 2 * share * (hidden // width)
+    shape = jax.ShapeDtypeStruct
+    return pl.pallas_call(
+        functools.partial(middle_kernel, len(pieces), share),
+        out_shape=(
+            shape((tokens, width), f32),
+            shape((tokens // 2, width), f32),
+            shape((tokens // 2, width), bf16),
+            shape((tokens, width), f32),
+            shape((tokens, width), bf16),
+            shape((1, hidden), f32),
+            shape((chips, rows, width), bf16),
+        ),
+        in_specs=[pl.BlockSpec(memory_space=SM)]
+        + [pl.BlockSpec(memory_space=VM)] * 9
+        + [pl.BlockSpec(memory_space=pl.ANY)] * len(pieces),
+        out_specs=[pl.BlockSpec(memory_space=VM)] * 6 + [pl.BlockSpec(memory_space=pl.ANY)],
+        scratch_shapes=[
+            VM((width, hidden), bf16),
+            VM((hidden, width), bf16),
+            VM((tokens, width), bf16),
+            VM((tokens, width), bf16),
+            VM((width, tokens), bf16),
+            VM((tokens // 2, width), f32),
+            VM((2, HALF_STEP, width), bf16),
+            VM((2, width, HALF_STEP), bf16),
+            pltpu.SemaphoreType.DMA,
+            pltpu.SemaphoreType.DMA((2,)),
+            pltpu.SemaphoreType.DMA((2,)),
+        ],
+        compiler_params=pltpu.CompilerParams(vmem_limit_bytes=56 * 1024 * 1024),
+        cost_estimate=pl.CostEstimate(
+            flops=12 * tokens * width * hidden, bytes_accessed=8 * width * hidden, transcendentals=tokens * hidden
+        ),
+        name="middle",
+    )(table, x_a, x_b, g_a, g_b, part, got_a, got_b, vectors, fc_bias, *pieces)
+
+
+def branch_kernel(count, share, row, table, resid, g_a, g_b, part, got_a, got_b, vectors, fc_sums, attn_in, *refs):
+    pieces = refs[:count]
+    given, grad_resid, sent, terms, w_out, branch, products, load_sem, sem = refs[count:]
+    f32, bf16 = jnp.float32, jnp.bfloat16
+    tokens, width = resid.shape
+    own = tokens // 2
+    chips, size, span = sent.shape
+    size -= 8
+    rows = span // 2
+
+    def targets(chip):
+        return [(pl.ds(0, share), w_out.at[rows_at(chip, share)])]
+
+    load_rows(table, pieces, targets, load_sem, False)
+    gain_sum = jnp.zeros((1, width), f32)
+    shift_sum = jnp.zeros((1, width), f32)
+    bias_sum = jnp.zeros((1, width), f32)
+    proj_sum = jnp.zeros((1, width), f32)
+    for half, (g_in, arrived) in enumerate(((g_a, got_a), (g_b, got_b))):
+        here = slice(half * own, (half + 1) * own)
+        value = resid[here, :]
+        centred = value - jnp.mean(value, axis=-1, keepdims=True)
+        inverse = lax.rsqrt(jnp.mean(centred * centred, axis=-1, keepdims=True) + 1e-05)
+        normed = centred * inverse
+        grad = part[here, :] + arrived[...].astype(f32)
+        gain_sum += jnp.sum(grad * normed, axis=0, keepdims=True)
+        shift_sum += jnp.sum(grad, axis=0, keepdims=True)
+        scaled = grad * vectors[0:1, :]
+        given_grad = g_in[...].astype(f32)
+        total = given_grad + inverse * (
+            scaled
+            - jnp.mean(scaled, axis=-1, keepdims=True)
+            - normed * jnp.mean(scaled * normed, axis=-1, keepdims=True)
+        )
+        rounded = total.astype(bf16)
+        bias_sum += jnp.sum(rounded.astype(f32), axis=0, keepdims=True)
+        proj_sum += jnp.sum(given_grad, axis=0, keepdims=True)
+        branch[here, :] = rounded
+        if half == 0:
+            grad_resid[...] = total
+    load_rows(table, pieces, targets, load_sem, True)
+    grads = dot_nt(w_out[...], branch[...]).astype(bf16)
+    group = width // (chips // 2)
+    sums = jnp.concatenate([gain_sum, shift_sum, bias_sum, proj_sum], axis=0)
+    each = fc_sums.shape[1] // chips
+    for chip in range(chips):
+        micro, head = divmod(chip, chips // 2)
+        for rel in range(2):
+            column = (rel * 2 + micro) * rows
+            sent[chip, :size, rel * rows : (rel + 1) * rows] = grads[
+                head * size : (head + 1) * size, column : column + rows
+            ]
+        first = chip // 2 * group
+        tail = jnp.concatenate(
+            [
+                sums[:, first : first + group],
+                fc_sums[:, chip * each : (chip + 1) * each],
+                jnp.zeros((3, group), f32),
+            ],
+            axis=0,
+        )
+        high = tail.astype(bf16)
+        low = (tail - high.astype(f32)).astype(bf16)
+        sent[chip, size:, :] = jnp.concatenate([high, low], axis=1)
+    products[...] = dot_nn(attn_in[...], branch[...]).astype(bf16)
+
+    @pl.loop(0, chips)
+    def _(chip):
+        pltpu.make_async_copy(products.at[rows_at(chip, share)], terms.at[table[1, chip], pl.ds(row, share)], sem).start()
+
+    @pl.loop(0, chips)
+    def _(chip):
+        pltpu.make_async_copy(products.at[rows_at(chip, share)], terms.at[table[1, chip], pl.ds(row, share)], sem).wait()
+
+
+def branch_back(table, resid, g_a, g_b, part, got_a, got_b, vectors, fc_sums, attn_in, pieces, terms, share, row, span):
+    tokens, width = resid.shape
+    f32, bf16 = jnp.float32, jnp.bfloat16
+    chips = table.shape[1]
+    size = attn_in.shape[0] // (chips // 2)
+    shape = jax.ShapeDtypeStruct
+    inputs = 10 + len(pieces)
+    return pl.pallas_call(
+        functools.partial(branch_kernel, len(pieces), share, row),
+        out_shape=(
+            shape((tokens // 2, width), f32),
+            shape((chips, size + 8, span), bf16),
+            shape(terms.shape, bf16),
+        ),
+        in_specs=[pl.BlockSpec(memory_space=SM)]
+        + [pl.BlockSpec(memory_space=VM)] * 9
+        + [pl.BlockSpec(memory_space=pl.ANY)] * (len(pieces) + 1),
+        out_specs=[pl.BlockSpec(memory_space=VM)] * 2 + [pl.BlockSpec(memory_space=pl.ANY)],
+        scratch_shapes=[
+            VM((chips * share, width), bf16),
+            VM((tokens, width), bf16),
+            VM((chips * share, width), bf16),
+            pltpu.SemaphoreType.DMA,
+            pltpu.SemaphoreType.DMA,
+        ],
+        input_output_aliases={inputs: 2},
+        compiler_params=pltpu.CompilerParams(vmem_limit_bytes=40 * 1024 * 1024),
+        cost_estimate=pl.CostEstimate(
+            flops=4 * tokens * chips * share * width, bytes_accessed=16 * tokens * width, transcendentals=0
+        ),
+        name="branch_back",
+    )(table, resid, g_a, g_b, part, got_a, got_b, vectors, fc_sums, attn_in, *pieces, terms)
+
+
+def finish_kernel(count, share, table, got, *refs):
+    pieces, (kept, sent, weight, grads, sem) = refs[:count], refs[count:]
+    chips, size, span = got.shape
+    rows = span // 2
+    own = kept.shape[0]
+
+    def targets(chip):
+        wanted = []
+        for core in range(2):
+            place = ((chip // 2) * 2 + core) * 2 + chip % 2
+            wanted.append((pl.ds(core * share, share), weight.at[rows_at(place, share)]))
+        return wanted
+
+    load_rows(table, pieces, targets, sem, False)
+    for chip in range(chips):
+        micro, head = divmod(chip, chips // 2)
+        for rel in range(2):
+            column = (rel * 2 + micro) * rows
+            grads[head * size : (head + 1) * size, column : column + rows] = got[chip, :, rel * rows : (rel + 1) * rows]
+    load_rows(table, pieces, targets, sem, True)
+    back = dot_nn(weight[...], grads[...])
+    kept[...] = back[:, :own].T
+    sent[...] = back[:, own:].T.astype(jnp.bfloat16)
+
+
+def finish(table, got, pieces, share):
+    chips, size, span = got.shape
+    depth = pieces[0].shape[2]
+    width = chips * 2 * share
+    bf16 = jnp.bfloat16
+    return pl.pallas_call(
+        functools.partial(finish_kernel, len(pieces), share),
+        out_shape=(
+            jax.ShapeDtypeStruct((span, width), jnp.float32),
+            jax.ShapeDtypeStruct((span, width), bf16),
+        ),
+        in_specs=[pl.BlockSpec(memory_space=SM), pl.BlockSpec(memory_space=VM)]
+        + [pl.BlockSpec(memory_space=pl.ANY)] * len(pieces),
+        out_specs=[pl.BlockSpec(memory_space=VM)] * 2,
+        scratch_shapes=[VM((width, depth), bf16), VM((depth, 2 * span), bf16), pltpu.SemaphoreType.DMA],
+        compiler_params=pltpu.CompilerParams(vmem_limit_bytes=32 * 1024 * 1024),
+        cost_estimate=pl.CostEstimate(
+            flops=4 * span * width * depth, bytes_accessed=2 * width * depth + 8 * span * width, transcendentals=0
+        ),
+        name="finish",
+    )(table, got, *pieces)
+
+
 PAIR = [(0, 1), (1, 0)]
-
-
-def swap(values, axis):
-    return lax.ppermute(values, axis, PAIR)
+NEAR = [(0, 1), (1, 0), (2, 3), (3, 2)]
+FAR = [(0, 2), (2, 0), (1, 3), (3, 1)]
+
+
+def swap(values, axis, pairs=PAIR):
+    return lax.ppermute(values, axis, pairs)
 
 
 def in_order(mine, other, index, axis):
     first = jnp.where(index == 0, mine, other)
     second = jnp.where(index == 0, other, mine)
     return jnp.stack([first, second], axis=axis)
-
-
-def shifted(values, count):
-    return [
-        lax.ppermute(values, "z", [(i, (i + step) % count) for i in range(count)]) for step in range(1, count)
-    ]
 
 
 def split_float(values):
@@ -698,6 +1082,13 @@
     low = jnp.where(runs == order[None, :], pair_start[None, :], 0)
     high = jnp.where(runs == 2 * pairs - 1 - order[None, :], pair_start[None, :] + 1, 0)
     return jnp.sum(low + high, axis=1).astype(jnp.int32)
+
+
+def ring_order(count):
+    half = [(z, (z + step) % 2) for z in range(count) for step in range(2)]
+    up = [(z * 2) * 2 + y for z, y in half]
+    down = [(z * 2 + 1) * 2 + y for z, y in reversed(half)]
+    return up + down
 
 
 def fast_body(
@@ -752,43 +1143,37 @@
     )
     high, low = split_float(offset)
     to_heads = jnp.concatenate([scaled_qkv, high[None], low[None], jnp.zeros((6, 3 * width), bf16)], axis=0)
-    to_heads = to_heads.reshape(share + 8, 3, heads, DH).transpose(2, 0, 1, 3).reshape(heads, 1, share + 8, 3 * DH)
-    to_heads = jnp.broadcast_to(to_heads, (heads, 2, share + 8, 3 * DH)).reshape(devices, share + 8, 3 * DH)
+    to_heads = to_heads.reshape(share + 8, 3, zx // 2, 2, 2, DH).transpose(2, 4, 3, 0, 1, 5)
+    to_heads = to_heads.reshape(1, heads, share + 8, 3 * DH)
+    to_heads = jnp.broadcast_to(to_heads, (2, heads, share + 8, 3 * DH)).reshape(devices, share + 8, 3 * DH)
     head_rows = lax.all_to_all(to_heads, every, split_axis=0, concat_axis=0, tiled=True)
     head_weight = head_rows[:, :share].reshape(width, 3 * DH)
     head_offset = jnp.sum(head_rows[:, share : share + 2].astype(f32), axis=(0, 1))
 
-    near = lax.dynamic_index_in_dim(n1, iy, 0, keepdims=False)
-    far = swap(lax.dynamic_index_in_dim(n1, 1 - iy, 0, keepdims=False), "head")
-    a_z = jnp.stack([near] + shifted(near, nz))
-    a_x = swap(a_z, "x")
-    b_x = jnp.stack([far, swap(far, "x")])
-    b_z = [b_x] + shifted(b_x, nz)
+    mine = iz // 2
+    near = lax.dynamic_index_in_dim(n1, mine, 0, keepdims=False)
+    far = swap(lax.dynamic_index_in_dim(n1, 1 - mine, 0, keepdims=False), "z", FAR)
+    near = jnp.stack([near, swap(near, "x")])
+    near = jnp.stack([near, swap(near, "z", NEAR)])
+    far = jnp.stack([far, swap(far, "head")])
+    far = jnp.stack([far, swap(far, "z", NEAR)])
+    parts = [near, swap(near, "head"), far, swap(far, "x")]
     pieces, owners = [], []
 
-    def add(piece, dz, dx, dy):
-        pieces.append(piece.reshape(-1, width))
-        owners.append((dz, dx, dy))
-
     def add_all(flip):
-        pick = (lambda v: swap(v, "core")) if flip else (lambda v: v)
         core = 1 - ic if flip else ic
-        for dx, part in enumerate((a_z, a_x)):
-            pieces.append(pick(part).reshape(-1, width))
-            owners.extend((dz, dx, core, 0) for dz in range(nz))
-        for dz, part in enumerate(b_z):
-            pieces.append(pick(part).reshape(-1, width))
-            owners.extend((dz, dx, core, 1) for dx in range(nx))
+        for index, part in enumerate(parts):
+            pieces.append((swap(part, "core") if flip else part).reshape(-1, width))
+            for dz in range(2):
+                for step in range(2):
+                    dx, dy = (step, index) if index < 2 else (index - 2, step)
+                    z = iz ^ dz if index < 2 else iz ^ dz ^ 2
+                    owners.append((z, ix ^ dx, core, iy ^ dy))
 
     add_all(False)
     add_all(True)
-    slot_device = jnp.stack(
-        [
-            (((iz - dz) % nz * nx + (ix + dx) % nx) * 2 + core) * 2 + (iy + dy) % 2
-            for dz, dx, core, dy in owners
-        ]
-    ).astype(jnp.int32)
-    my_dealt = lax.dynamic_index_in_dim(dealt, iy, 0, keepdims=False)
+    slot_device = jnp.stack([((z * nx + x) * 2 + core) * 2 + y for z, x, core, y in owners]).astype(jnp.int32)
+    my_dealt = lax.dynamic_index_in_dim(dealt, mine, 0, keepdims=False)
     order = my_dealt.reshape(devices, rows)[:, 0] // RUN
     slot_of = jnp.sum(
         jnp.where(jnp.arange(devices)[:, None] == slot_device[None, :], jnp.arange(devices)[None, :], 0), axis=1
@@ -798,7 +1183,7 @@
     id_y, id_c, id_zx = ids % 2, ids // 2 % 2, ids // 4
     send_pair = (id_zx * 2 + id_y) * 2 + (id_c ^ ic)
     outloc = run_table(order, (send_pair * 2).astype(jnp.int32))
-    bound = lax.dynamic_index_in_dim(lengths, iy, 0, keepdims=False)[:1]
+    bound = lax.dynamic_index_in_dim(lengths, mine, 0, keepdims=False)[:1]
 
     fc_parts = fc_weight.reshape(share, zx, 2, 2, hidden_share)
 
@@ -816,19 +1201,13 @@
     folds = hidden_half // width
     fc_folded = fc_pair.reshape(2 * share, folds, width).transpose(1, 0, 2).reshape(-1, width)
     packed = jnp.concatenate([out_weight, proj_weight, fc_folded, small_row], axis=0)
-    gathered = lax.all_gather(packed, chips, axis=0)
+    ring = ring_order(nz)
+    places = [ring.index(chip) for chip in range(chip_count)]
+    table = jnp.array([ring, places], jnp.int32)
+    gathered = lax.all_gather(packed, chips, axis=0, axis_index_groups=[ring])
     out_rows = share
     proj_rows = hidden_share
     fc_rows = 2 * share * folds
-    w_out = gathered[:, :out_rows].reshape(local, width)
-    w_proj = gathered[:, out_rows : out_rows + proj_rows].reshape(hidden_half, width)
-    w_fc = gathered[:, out_rows + proj_rows : out_rows + proj_rows + fc_rows]
-    w_fc = w_fc.reshape(zx, 2, folds, 2, share, width).transpose(0, 3, 1, 4, 2, 5).reshape(width, hidden_half)
-    smalls = gathered[:, out_rows + proj_rows + fc_rows :].reshape(chip_count, 8 * width)
-    vectors = smalls[:, : 8 * share].astype(f32).reshape(zx, 2, 2, 4, share)
-    vectors = vectors.transpose(3, 0, 2, 1, 4).reshape(4, width)
-    gain_two, shift_two, b_out, b_proj = vectors[0], vectors[1], vectors[2], vectors[3]
-    b_fc = smalls[:, 8 * share : 8 * share + hidden_share].astype(f32).reshape(hidden_half)
 
     qkv_parts = scaled_qkv.reshape(share, 3, zx, 2, DH).transpose(0, 2, 1, 3, 4)
 
@@ -836,78 +1215,55 @@
         return lax.dynamic_index_in_dim(qkv_parts, index, 3, keepdims=False).reshape(share, 3 * local)
 
     qkv_pair = in_order(core_heads(ic), swap(core_heads(1 - ic), "core"), ic, 0)
-    packed_qkv, gathered, head_rows = lax.optimization_barrier((qkv_pair, gathered, head_rows))
-    w_qkv = lax.all_gather(packed_qkv, chips, axis=0)
-    w_qkv = w_qkv.reshape(zx, 2, 2, share, 3 * local).transpose(0, 2, 1, 3, 4).reshape(width, 3 * local)
 
     mixed = [(product(piece, head_weight) + head_offset).astype(bf16) for piece in pieces]
     slots = jnp.concatenate(mixed, axis=0)
     attn_send, queries, keys, values, attn_t, lse = attend_forward(bound, inloc, outloc, slots, chip_count, DH)
 
-    x_all = jnp.stack([block_input, swap(block_input, "core")]).reshape(-1, width)
-    g_all = jnp.stack([out_grad, swap(out_grad, "core")]).reshape(-1, width)
+    x_a, x_b = block_input.reshape(-1, width), swap(block_input, "core").reshape(-1, width)
+    g_a, g_b = out_grad.reshape(-1, width), swap(out_grad, "core").reshape(-1, width)
     own = micro * rows
-    grad_hidden = product_nt(g_all, w_proj)
-
     attn_got = lax.all_to_all(attn_send, chips, split_axis=0, concat_axis=0, tiled=True)
-    attn_in = attn_got.reshape(zx, 2, DH, 2, rows).transpose(0, 2, 3, 1, 4).reshape(local, 2 * own)
-
-    def share_sum(part):
-        sent = part.astype(bf16)
-        first = swap(sent[own:], "core")
-        second = swap(sent[:own], "core")
-        return part + jnp.concatenate([first, second], axis=0).astype(f32)
-
-    resid = x_all.astype(f32) + share_sum(product_tn(attn_in, w_out)) + b_out
-    normed_two, inverse_two = normalize(resid)
-    act_two = (normed_two * gain_two + shift_two).astype(bf16)
-    pre = product(act_two, w_fc) + b_fc
-    hidden, gelu_back = jax.vjp(gelu_tanh, pre)
-    hidden = hidden.astype(bf16)
-    projected = product(hidden, w_proj)
-    project_other = swap(projected[own:].astype(bf16), "core")
-    output = (resid[:own] + projected[:own] + project_other.astype(f32) + b_proj).astype(bf16)
-
-    grad_pre = gelu_back(grad_hidden)[0].astype(bf16)
-    grad_proj_w = product_tn(hidden, g_all).astype(bf16)
-    grad_fc_w = product_tn(act_two, grad_pre).astype(bf16)
-    grad_fc_b = jnp.sum(grad_pre.astype(f32), axis=0)
-    grad_proj_b = jnp.sum(g_all.astype(f32), axis=0)
-    grad_act_two = share_sum(product_nt(grad_pre, w_fc))
-    grad_gain_two = jnp.sum(grad_act_two * normed_two, axis=0)
-    grad_shift_two = jnp.sum(grad_act_two, axis=0)
-    grad_resid = g_all.astype(f32) + norm_back(grad_act_two * gain_two, normed_two, inverse_two)
-    grad_branch = grad_resid.astype(bf16)
-    grad_out_b = jnp.sum(grad_branch.astype(f32), axis=0)
-    grad_out_w = product(attn_in, grad_branch).astype(bf16)
-    grad_attn = product_nt(w_out, grad_branch).astype(bf16)
-
-    sums = jnp.stack([grad_gain_two, grad_shift_two, grad_out_b, grad_proj_b]).reshape(4, zx, 2, 2, share)
-    sums = lax.dynamic_index_in_dim(sums, ic, 2, keepdims=False).transpose(1, 2, 0, 3).reshape(chip_count, 4 * share)
-    sums = jnp.concatenate([sums, grad_fc_b.reshape(chip_count, hidden_share)], axis=1)
-    high, low = split_float(sums)
-    extra = jnp.stack([high, low], axis=1)
-    extra = jnp.pad(extra, ((0, 0), (0, 6), (0, 2 * rows - extra.shape[2])))
-    grad_send = grad_attn.reshape(zx, DH, 2, 2, rows).transpose(0, 3, 1, 2, 4).reshape(chip_count, DH, 2 * rows)
-    grad_got = lax.all_to_all(
-        jnp.concatenate([grad_send, extra], axis=1), chips, split_axis=0, concat_axis=0, tiled=True
-    )
+    gathered, qkv_pair, _ = lax.optimization_barrier((gathered, qkv_pair, lse))
+    qkv_pair = qkv_pair.reshape(2 * share, 3 * local)
+    w_qkv = lax.all_gather(qkv_pair, chips, axis=0, axis_index_groups=[ring])
+    smalls = gathered[:, out_rows + proj_rows + fc_rows :].reshape(chip_count, 8 * width)
+    smalls = jnp.stack([smalls[place] for place in places])
+    vectors = smalls[:, : 8 * share].astype(f32).reshape(zx, 2, 2, 4, share)
+    vectors = jnp.pad(vectors.transpose(3, 0, 2, 1, 4).reshape(4, width), ((0, 4), (0, 0)))
+    b_fc = smalls[:, 8 * share : 8 * share + hidden_share].astype(f32).reshape(1, hidden_half)
+    part, sent, attn_in = project(table, attn_got, [gathered], share)
+    resid, base, project_other, grad_part, sent_back, fc_sums, terms = middle(
+        table, x_a, x_b, g_a, g_b, part, swap(sent[own:], "core"), swap(sent[:own], "core"), vectors, b_fc, [gathered], share
+    )
+    grad_resid, grad_send, terms = branch_back(
+        table,
+        resid,
+        g_a,
+        g_b,
+        grad_part,
+        swap(sent_back[own:], "core"),
+        swap(sent_back[:own], "core"),
+        vectors,
+        fc_sums,
+        attn_in,
+        [gathered],
+        terms,
+        share,
+        proj_rows,
+        2 * rows,
+    )
+    output = (base + swap(project_other, "core").astype(f32)).astype(bf16)
+
+    grad_got = lax.all_to_all(grad_send, chips, split_axis=0, concat_axis=0, tiled=True)
     grad_heads = grad_got[:, :DH]
-    vector_sums = jnp.sum(grad_got[:, DH : DH + 2].astype(f32), axis=(0, 1))
-    final_vectors = vector_sums[: 4 * share].reshape(4, share)
-    final_fc_b = vector_sums[4 * share : 4 * share + hidden_share]
-
-    final_proj_w = lax.psum_scatter(grad_proj_w, chips, scatter_dimension=0, tiled=True).astype(f32)
-    fc_terms = grad_fc_w.reshape(zx, 2, 2, share, hidden_half).transpose(0, 2, 1, 3, 4).reshape(width, hidden_half)
-    fc_sum = lax.psum_scatter(fc_terms, chips, scatter_dimension=0, tiled=True).reshape(2, share, hidden_half)
-    final_out_w = lax.psum_scatter(grad_out_w, chips, scatter_dimension=0, tiled=True).astype(f32)
-    fc_keep = lax.dynamic_index_in_dim(fc_sum, ic, 0, keepdims=False)
-    fc_give = swap(lax.dynamic_index_in_dim(fc_sum, 1 - ic, 0, keepdims=False), "core")
-    final_fc_w = in_order(
-        fc_keep.reshape(share, zx, 2, hidden_share), fc_give.reshape(share, zx, 2, hidden_share), ic, 2
-    )
-    final_fc_w = final_fc_w.reshape(share, 2 * hidden_half).astype(f32)
-
+    vector_sums = jnp.sum(grad_got[:, DH:].astype(f32), axis=0)
+    vector_sums = vector_sums[:, :rows] + vector_sums[:, rows:]
+    final_vectors = lax.dynamic_slice(vector_sums, (0, (ic * 2 + iy) * share), (4, share))
+    final_fc_b = vector_sums[4]
+
+    summed = lax.psum_scatter(terms, chips, scatter_dimension=0, tiled=True, axis_index_groups=[ring])[0]
+    final_proj_w = summed[:proj_rows].astype(f32)
     slot_grads, send_grads = attend_backward(
         bound, inloc, outloc, grad_heads, queries, keys, values, attn_t, lse
     )
@@ -921,29 +1277,43 @@
     column_sums = jnp.sum(slot_grads.astype(f32), axis=0)
     high, low = split_float(column_sums)
     tail = jnp.concatenate([high[None], low[None], jnp.zeros((6, 3 * DH), bf16)], axis=0)
+    raw_rows = raw_term.astype(bf16).reshape(zx, 2, 2, share, 3 * DH).transpose(0, 2, 1, 3, 4)
     raw_send = jnp.concatenate(
         [
-            raw_term.astype(bf16).reshape(devices, share, 3 * DH),
-            jnp.broadcast_to(tail[None], (devices, 8, 3 * DH)),
+            raw_rows.reshape(chip_count, 2 * share, 3 * DH),
+            jnp.broadcast_to(tail[None], (chip_count, 8, 3 * DH)),
         ],
         axis=1,
     )
-    raw_got = lax.all_to_all(raw_send, every, split_axis=0, concat_axis=0, tiled=True)
-    raw_sum = jnp.sum(raw_got.reshape(heads, 2, share + 8, 3 * DH).astype(f32), axis=1)
-    raw_grad = raw_sum[:, :share].reshape(heads, share, 3, DH).transpose(1, 2, 0, 3).reshape(share, 3 * width)
-    all_sums = (raw_sum[:, share] + raw_sum[:, share + 1]).reshape(heads, 3, DH).transpose(1, 0, 2)
-    all_sums = all_sums.reshape(3 * width)
+    raw_send, grads_got = lax.optimization_barrier((raw_send, grads_got))
+    final_out_w = summed[proj_rows : proj_rows + out_rows].astype(f32)
+    fc_sum = summed[proj_rows + out_rows :].reshape(folds, 2, share, width)
+    fc_keep = lax.dynamic_index_in_dim(fc_sum, ic, 1, keepdims=False)
+    fc_give = swap(lax.dynamic_index_in_dim(fc_sum, 1 - ic, 1, keepdims=False), "core")
+
+    def by_owner(values):
+        return values.transpose(1, 0, 2).reshape(share, zx, 2, hidden_share)
+
+    final_fc_w = in_order(by_owner(fc_keep), by_owner(fc_give), ic, 2).reshape(share, 2 * hidden_half).astype(f32)
+    raw_got = lax.all_to_all(raw_send, chips, split_axis=0, concat_axis=0, tiled=True)
+    raw_sum = jnp.sum(raw_got.reshape(2, zx, 2 * share + 8, 3 * DH).astype(f32), axis=0)
+    raw_parts = raw_sum[:, : 2 * share].reshape(zx, 2, share, 3 * DH)
+    sums_mine = raw_sum[:, 2 * share : 2 * share + 1] + raw_sum[:, 2 * share + 1 : 2 * share + 2]
+    raw_keep = jnp.concatenate([lax.dynamic_index_in_dim(raw_parts, ic, 1, keepdims=False), sums_mine], axis=1)
+    raw_give = jnp.concatenate([lax.dynamic_index_in_dim(raw_parts, 1 - ic, 1, keepdims=False), sums_mine], axis=1)
+    raw_all = in_order(raw_keep, swap(raw_give, "core"), ic, 1).reshape(heads, share + 1, 3, DH)
+    raw_all = raw_all.transpose(1, 2, 0, 3).reshape(share + 1, 3 * width)
+    raw_grad, all_sums = raw_all[:share], raw_all[share]
     final_qkv_w = raw_grad * gain_one[:, None] + shift_one[:, None] * all_sums[None, :]
     final_gain_one = jnp.sum(raw_grad * raw_qkv, axis=1)
     final_shift_one = jnp.sum(raw_qkv * all_sums[None, :], axis=1)
     final_q_b = lax.dynamic_slice(all_sums, (place,), (share,))
     final_v_b = lax.dynamic_slice(all_sums, (2 * width + place,), (share,))
 
-    grads_in = grads_got.reshape(zx, 2, 3 * DH, 2, rows).transpose(0, 2, 3, 1, 4).reshape(3 * local, 2 * own)
-    back = lax.dot_general(grads_in, w_qkv, (((0,), (1,)), ((), ())), preferred_element_type=f32)
-    back_own = back[:own] + swap(back[own:].astype(bf16), "core").astype(f32)
+    back_own, back_other = finish(table, grads_got, [w_qkv], share)
+    back_own = back_own + swap(back_other, "core").astype(f32)
     back_own = back_own.reshape(micro, rows, width)
-    input_grad = grad_resid[:own].reshape(micro, rows, width) + norm_back(back_own, normed_one, inverse_one)
+    input_grad = grad_resid.reshape(micro, rows, width) + norm_back(back_own, normed_one, inverse_one)
 
     return (
         output.reshape(micro, rows, width),

time: 631 us -> 449 us (0.71)
  waiting for transfers between devices: 314 us -> 176 us
  Pallas kernels: 55.9 us -> 98.5 us
  matrix products: 53.8 us -> 15.8 us
  local copies, waits for them, and re-layouts: 76.3 us -> 44.7 us
    reduce_scatter x3 -> x1, waiting for transfers between devices: 139 us -> 0.01 us  [fast_body(): lax.psum_scatter(terms, chips, scatter_dimension=0, tiled=True, axis_inde...]
    ppermute x27 -> x24, waiting for transfers between devices: 131 us -> 86.2 us  [swap(): return lax.ppermute(values, axis, pairs)]
    pallas_call x0 -> x4, Pallas kernels: none -> 42.7 us  [the longest x1 26.6 us: middle(): pl.pallas_call(functools.partial(middle_kernel, len(pieces), share), out_...]
    all_to_all x2, waiting for transfers between devices: 6.77 us -> 34.9 us  [the longest x1 18.5 us: fast_body(): lax.all_to_all(grad_send, chips, split_axis=0, concat_axis=0, tiled=True)]
    reshape x14 -> x4, local copies, waits for them, and re-layouts: 21.5 us -> 0.92 us  [the longest x1 0.7 us: fast_body(): in_order(raw_keep, swap(raw_give, 'core'), ic, 1)]
    dot_general x4 -> x0, matrix products: 13.6 us -> none  [the longest x3 11.7 us: product_nt(): lax.dot_general(left, right, (((1,), (1,)), ((), ())), preferred_element_...]
    dot_general x15 -> x8, matrix products: 21.1 us -> 8.59 us  [product_tn(): lax.dot_general(left, right, (((0,), (0,)), ((), ())), preferred_element_...]
    dot_general x15 -> x8, matrix products: 19.2 us -> 7.21 us  [product(): return jnp.dot(left, right, preferred_element_type=jnp.float32)]
  transfers between devices with their start and end apart: 37 -> 32, of which waited for: 13 -> 10; matrix products, arithmetic and copies ran while one was open for 24% -> 15% of each run, Pallas kernels for 9% -> 22%
where the time goes in v2:
time: 449 us; the launch traced here: 442 us
  waiting for transfers between devices  176 us (39%)
  Pallas kernels  98.5 us (22%)
  starting transfers between devices  62.9 us (14%)
  local copies, waits for them, and re-layouts  44.7 us (10%)
  other arithmetic  29.5 us (7%)
  matrix products  15.8 us (4%)
  between operations  15.3 us (3%)
    ppermute x24, waiting for transfers between devices, swap(): return lax.ppermute(values, axis, pairs)  86.2 us
    all_to_all x1, waiting for transfers between devices, fast_body(): lax.all_to_all(send_grads, chips, split_axis=0, concat_axis=0, tiled=True)  38.1 us
    pallas_call x1, Pallas kernels, attend_backward(): pl.pallas_call(functools.partial(backward_kernel, head_size), out_shape=(...  30.5 us
    pallas_call x1, Pallas kernels, middle(): pl.pallas_call(functools.partial(middle_kernel, len(pieces), share), out_...  26.6 us
    pallas_call x1, Pallas kernels, attend_forward(): pl.pallas_call(functools.partial(forward_kernel, head_size), out_shape=(j...  25.2 us
    unnamed x107, local copies, waits for them, and re-layouts  24.8 us
    ppermute x24, starting transfers between devices, swap(): return lax.ppermute(values, axis, pairs)  21.1 us
    all_to_all x1, waiting for transfers between devices, fast_body(): lax.all_to_all(grad_send, chips, split_axis=0, concat_axis=0, tiled=True)  18.5 us
  transfers between devices with their start and end apart: 32, of which 10 were waited for; matrix products, arithmetic and copies ran while one was open for 15% of the time, Pallas kernels for 22%

profile of v2, /device:TPU:11, one launch (start us, length us, event | category | flops | bytes accessed | tf_op | source)
XLA Modules:
  0.0 442.2 jit_solution(6999350772773836305)
XLA Ops:
  21.3 6.5 %all-to-all-start = ((bf16[32,40,192]{2,1,0:T(8,128)(2,1)}), bf16[32,40,192]{2,1,0:T(8,128)(2,1)S(1)}, u32[]{:S(2)}, u32[]{:S(2)}) async-start(bf16[32,40,192]{2,1,0:T(8,128)(2,1)} %bitcast.44), calls=%async_computation | async-start | bytes 1310720 | tf_op jit(solution)/shard_map/all_to_all | solution.py:1149
  34.2 32.2 %collective-permute-done.5 = bf16[128,1024]{1,0:T(8,128)(2,1)} collective-permute-done((bf16[128,1024]{1,0:T(8,128)(2,1)}, bf16[128,1024]{1,0:T(8,128)(2,1)}, u32[]{:S(2)}, u32[]{:S(2)}) %collective-permute-start.5) | collective-permute-done | bytes 262176 | tf_op jit(solution)/shard_map/ppermute | solution.py:1064
  66.9 11.8 %collective-permute-done.6 = bf16[128,1024]{1,0:T(8,128)(2,1)S(1)} collective-permute-done((bf16[128,1024]{1,0:T(8,128)(2,1)}, bf16[128,1024]{1,0:T(8,128)(2,1)S(1)}, u32[]{:S(2)}, u32[]{:S(2)}) %collective-permute-start.6) | collective-permute-done | bytes 262176 | tf_op jit(solution)/shard_map/ppermute | solution.py:1064
  79.7 3.0 collective-permute-start.7
  82.9 9.8 %collective-permute-done.7 = bf16[2,128,1024]{2,1,0:T(8,128)(2,1)S(1)} collective-permute-done((bf16[2,128,1024]{2,1,0:T(8,128)(2,1)S(1)}, bf16[2,128,1024]{2,1,0:T(8,128)(2,1)S(1)}, u32[]{:S(2)}, u32[]{:S(2)}) %collective-permute-start.7) | collective-permute-done | bytes 524320 | tf_op jit(solution)/shard_map/ppermute | solution.py:1064
  94.4 3.0 collective-permute-start.9
  98.0 30.2 %collective-permute-done.4 = bf16[2,2,128,1024]{3,2,1,0:T(8,128)(2,1)} collective-permute-done((bf16[2,2,128,1024]{3,2,1,0:T(8,128)(2,1)S(1)}, bf16[2,2,128,1024]{3,2,1,0:T(8,128)(2,1)}, u32[]{:S(2)}, u32[]{:S(2)}) %collective-permute-start.4) | collective-permute-done | bytes 1048608 | tf_op jit(solution)/shard_map/ppermute | solution.py:1064
  128.2 4.1 collective-permute-start.10
  139.9 25.2 %attend_forward.1 = (bf16[16,64,256]{2,1,0:T(8,128)(2,1)}, bf16[4096,64]{1,0:T(8,128)(2,1)S(1)}, bf16[4096,64]{1,0:T(8,128)(2,1)S(1)}, bf16[4096,64]{1,0:T(8,128...) custom-call(s32[1]{0:T(128)S(1)} %bitcast.248, s32[64]{0:T(128)S(1)} %get-tuple-element.72.inloc, ...), custom_call_target="tpu_custom_call" | custom-call | flops 8589934592 | bytes 8388608 | tf_op jit(solution)/shard_map/attend_forward/pallas_call | solution.py:544
  168.1 12.4 %all-to-all-start.1 = ((bf16[16,64,256]{2,1,0:T(8,128)(2,1)}), bf16[16,64,256]{2,1,0:T(8,128)(2,1)S(1)}, u32[]{:S(2)}, u32[]{:S(2)}) async-start(bf16[16,64,256]{2,1,0:T(8,128)(2,1)} %get-tuple-element.42), calls=%async_computation.1 | async-start | bytes 1048576 | tf_op jit(solution)/shard_map/all_to_all | solution.py:1226
  181.4 16.3 %all-to-all-done.1.got = bf16[16,64,256]{2,1,0:T(8,128)(2,1)S(1)} async-done(((bf16[16,64,256]{2,1,0:T(8,128)(2,1)}), bf16[16,64,256]{2,1,0:T(8,128)(2,1)S(1)}, u32[]{:S(2)}, u32[]{:S(2)}) %all-to-all-start.1) | async-done | bytes 524320 | tf_op jit(solution)/shard_map/all_to_all | solution.py:1226
  197.7 3.8 copy-done.2
  201.5 3.0 project.1
  214.2 2.4 stack.250
  218.9 26.6 %middle.1 = (f32[512,1024]{1,0:T(8,128)}, f32[256,1024]{1,0:T(8,128)}, bf16[256,1024]{1,0:T(8,128)(2,1)}, f32[512,1024]{1,0:T(8,128)}, bf16[512,1024]{1,0:T(8,12...) custom-call(s32[2,16]{1,0:T(2,128)} %constant.161.clone.table, bf16[256,1024]{1,0:T(8,128)(2,1)} %bitcast.x_a, ...), custom_call_target="tpu_custom_call" | custom-call | flops 12884901888 | bytes 16777216 | tf_op jit(solution)/shard_map/middle/pallas_call | solution.py:865
  252.7 5.9 %branch_back.1 = (f32[256,1024]{1,0:T(8,128)S(1)}, bf16[16,72,256]{2,1,0:T(8,128)(2,1)}, bf16[16,288,1024]{2,1,0:T(8,128)(2,1)}) custom-call(s32[2,16]{1,0:T(2,128)S(1)} %copy-done.14, f32[512,1024]{1,0:T(8,128)S(1)} %copy-done.3, bf16[256,1024]{1,0:T(8,128)(2,1)S(1)} %bitcast.245, ...), custom_call_target="tpu_custom_call", output_to_operand_aliasing={{2}: (11, {})} | custom-call | flops 1073741824 | bytes 8388608 | tf_op jit(solution)/shard_map/branch_back/pallas_call | solution.py:983
  259.7 7.9 %all-to-all-start.2 = ((bf16[16,72,256]{2,1,0:T(8,128)(2,1)}), bf16[16,72,256]{2,1,0:T(8,128)(2,1)S(1)}, u32[]{:S(2)}, u32[]{:S(2)}) async-start(bf16[16,72,256]{2,1,0:T(8,128)(2,1)} %get-tuple-element.56), calls=%async_computation.2 | async-start | bytes 1179648 | tf_op jit(solution)/shard_map/all_to_all | solution.py:1258
  268.6 18.5 %all-to-all-done.2 = bf16[16,72,256]{2,1,0:T(8,128)(2,1)S(1)} async-done(((bf16[16,72,256]{2,1,0:T(8,128)(2,1)}), bf16[16,72,256]{2,1,0:T(8,128)(2,1)S(1)}, u32[]{:S(2)}, u32[]{:S(2)}) %all-to-all-start.2) | async-done | bytes 589856 | tf_op jit(solution)/shard_map/all_to_all | solution.py:1258
  288.4 30.5 %attend_backward.1 = (bf16[4096,192]{1,0:T(8,128)(2,1)}, bf16[16,192,256]{2,1,0:T(8,128)(2,1)}) custom-call(s32[1]{0:T(128)S(1)} %bitcast.249, s32[64]{0:T(128)S(1)} %get-tuple-element.72.inloc, s32[64]{0:T(128)S(1)} %get-tuple-element.71.outloc, bf16[16,64,256]{2,1,0:T(8,128)(2,1)S(1)} %slice.302.grad_t, bf16[4096,64]{1,0:T(8,128)(2,1)S(1)} %copy-done.18, ...), custom_call_target="tpu_custom_call" | custom-call | flops 21474836480 | bytes 16777216 | tf_op jit(solution)/shard_map/attend_backward/pallas_call | solution.py:647
  319.0 6.9 %all-to-all-start.3 = ((bf16[16,192,256]{2,1,0:T(8,128)(2,1)}), bf16[16,192,256]{2,1,0:T(8,128)(2,1)S(1)}, u32[]{:S(2)}, u32[]{:S(2)}) async-start(bf16[16,192,256]{2,1,0:T(8,128)(2,1)} %get-tuple-element.62), calls=%async_computation.3 | async-start | bytes 3145728 | tf_op jit(solution)/shard_map/all_to_all | solution.py:1270
  339.0 38.1 %all-to-all-done.3.got = bf16[16,192,256]{2,1,0:T(8,128)(2,1)S(1)} async-done(((bf16[16,192,256]{2,1,0:T(8,128)(2,1)}), bf16[16,192,256]{2,1,0:T(8,128)(2,1)S(1)}, u32[]{:S(2)}, u32[]{:S(2)}) %all-to-all-start.3) | async-done | bytes 1572896 | tf_op jit(solution)/shard_map/all_to_all | solution.py:1270
  377.1 7.2 %all-to-all-start.4 = ((bf16[16,72,192]{2,1,0:T(8,128)(2,1)}), bf16[16,72,192]{2,1,0:T(8,128)(2,1)S(1)}, u32[]{:S(2)}, u32[]{:S(2)}) async-start(bf16[16,72,192]{2,1,0:T(8,128)(2,1)} %pad_maximum_fusion.3), calls=%async_computation.4 | async-start | bytes 1179648 | tf_op jit(solution)/shard_map/all_to_all | solution.py:1298
  387.3 16.4 %all-to-all-done.4 = bf16[16,72,192]{2,1,0:T(8,128)(2,1)S(1)} async-done(((bf16[16,72,192]{2,1,0:T(8,128)(2,1)}), bf16[16,72,192]{2,1,0:T(8,128)(2,1)S(1)}, u32[]{:S(2)}, u32[]{:S(2)}) %all-to-all-start.4) | async-done | bytes 442400 | tf_op jit(solution)/shard_map/all_to_all | solution.py:1298
  409.0 7.2 %finish.1 = (f32[256,1024]{1,0:T(8,128)S(1)}, bf16[256,1024]{1,0:T(8,128)(2,1)S(1)}) custom-call(s32[2,16]{1,0:T(2,128)S(1)} %copy-done.14, bf16[16,192,256]{2,1,0:T(8,128)(2,1)S(1)} %all-to-all-done.3.got, bf16[16,64,1536]{2,1,0:T(8,128)(2,1)S(1)} %copy-done.15), custom_call_target="tpu_custom_call" | custom-call | flops 1610612736 | bytes 5242880 | tf_op jit(solution)/shard_map/finish/pallas_call | solution.py:1040
  (302 shorter events, 98.0 us)
Async XLA Ops:
  7.2 160.9 %all-gather.6.cloned.1.call-start = ((), (), s32[]{:S(2)}) async-start(), calls=%async_computation.8 | async-start | bytes 10305536 | tf_op jit(solution)/shard_map/all_gather | solution.py:1207
  17.8 16.0 %collective-permute-start.2 = (bf16[128,1024]{1,0:T(8,128)(2,1)S(1)}, bf16[128,1024]{1,0:T(8,128)(2,1)S(1)}, u32[]{:S(2)}, u32[]{:S(2)}) collective-permute-start(bf16[128,1024]{1,0:T(8,128)(2,1)S(1)} %bitcast.270), channel_id=1, source_target_pairs={{0,2},{2,0},{1,3},{3,1},{4,6},{6,4},{5,7},{7,5},{8,10},{10,8},{9,1... | collective-permute-start | bytes 786440 | tf_op jit(solution)/shard_map/ppermute | solution.py:1064
  21.3 76.0 %all-to-all-start = ((bf16[32,40,192]{2,1,0:T(8,128)(2,1)}), bf16[32,40,192]{2,1,0:T(8,128)(2,1)S(1)}, u32[]{:S(2)}, u32[]{:S(2)}) async-start(bf16[32,40,192]{2,1,0:T(8,128)(2,1)} %bitcast.44), calls=%async_computation | async-start | bytes 1310720 | tf_op jit(solution)/shard_map/all_to_all | solution.py:1149
  27.8 379.3 %all-gather.4.cloned.1.call-start = ((), (), s32[]{:S(2)}) async-start(), calls=%async_computation.6 | async-start | bytes 3342336 | tf_op jit(solution)/shard_map/all_gather | solution.py:1229
  28.4 38.0 %collective-permute-start.5 = (bf16[128,1024]{1,0:T(8,128)(2,1)}, bf16[128,1024]{1,0:T(8,128)(2,1)}, u32[]{:S(2)}, u32[]{:S(2)}) collective-permute-start(bf16[128,1024]{1,0:T(8,128)(2,1)} %get-tuple-element.107), channel_id=1, source_target_pairs={{0,8},{8,0},{4,12},{12,4},{1,9},{9,1},{5,13},{13,5},{2,10},{10,2},... | collective-permute-start | bytes 786440 | tf_op jit(solution)/shard_map/ppermute | solution.py:1064
  32.8 50.1 %collective-permute-start.15 = (bf16[32,1536]{1,0:T(8,128)(2,1)}, bf16[32,1536]{1,0:T(8,128)(2,1)S(1)}, u32[]{:S(2)}, u32[]{:S(2)}) collective-permute-start(bf16[32,1536]{1,0:T(8,128)(2,1)} %reshape.486), channel_id=1, source_target_pairs={{0,1},{1,0},{2,3},{3,2},{4,5},{5,4},{6,7},{7,6},{8,9},{9,8},{10,11... | collective-permute-start | bytes 294920 | tf_op jit(solution)/shard_map/ppermute | solution.py:1064
  33.9 48.8 %collective-permute-start.3 = (bf16[2,128,1024]{2,1,0:T(8,128)(2,1)S(1)}, bf16[2,128,1024]{2,1,0:T(8,128)(2,1)S(1)}, u32[]{:S(2)}, u32[]{:S(2)}) collective-permute-start(bf16[2,128,1024]{2,1,0:T(8,128)(2,1)S(1)} %get-tuple-element.110), channel_id=1, source_target_pairs={{0,4},{4,0},{8,12},{12,8},{1,5},{5,1},{9,13},{13,9},{2,6},{6,2},{1... | collective-permute-start | bytes 1572872 | tf_op jit(solution)/shard_map/ppermute | solution.py:1064
  66.4 12.3 %collective-permute-start.6 = (bf16[128,1024]{1,0:T(8,128)(2,1)}, bf16[128,1024]{1,0:T(8,128)(2,1)S(1)}, u32[]{:S(2)}, u32[]{:S(2)}) collective-permute-start(bf16[128,1024]{1,0:T(8,128)(2,1)} %collective-permute-done.5), channel_id=1, source_target_pairs={{0,16},{16,0},{1,17},{17,1},{2,18},{18,2},{3,19},{19,3},{4,20},{20... | collective-permute-start | bytes 786440 | tf_op jit(solution)/shard_map/ppermute | solution.py:1064
  79.7 13.0 %collective-permute-start.7 = (bf16[2,128,1024]{2,1,0:T(8,128)(2,1)S(1)}, bf16[2,128,1024]{2,1,0:T(8,128)(2,1)S(1)}, u32[]{:S(2)}, u32[]{:S(2)}) collective-permute-start(bf16[2,128,1024]{2,1,0:T(8,128)(2,1)S(1)} %get-tuple-element.106), channel_id=1, source_target_pairs={{0,4},{4,0},{8,12},{12,8},{1,5},{5,1},{9,13},{13,9},{2,6},{6,2},{1... | collective-permute-start | bytes 1572872 | tf_op jit(solution)/shard_map/ppermute | solution.py:1064
  82.8 45.4 %collective-permute-start.4 = (bf16[2,2,128,1024]{3,2,1,0:T(8,128)(2,1)S(1)}, bf16[2,2,128,1024]{3,2,1,0:T(8,128)(2,1)}, u32[]{:S(2)}, u32[]{:S(2)}) collective-permute-start(bf16[2,2,128,1024]{3,2,1,0:T(8,128)(2,1)S(1)} %pad_maximum_fusion), channel_id=1, source_target_pairs={{0,16},{16,0},{1,17},{17,1},{2,18},{18,2},{3,19},{19,3},{4,20},{20... | collective-permute-start | bytes 3145736 | tf_op jit(solution)/shard_map/ppermute | solution.py:1064
  92.9 41.6 %collective-permute-start.8 = (bf16[2,2,128,1024]{3,2,1,0:T(8,128)(2,1)S(1)}, bf16[2,2,128,1024]{3,2,1,0:T(8,128)(2,1)}, u32[]{:S(2)}, u32[]{:S(2)}) collective-permute-start(bf16[2,2,128,1024]{3,2,1,0:T(8,128)(2,1)S(1)} %pad_maximum_fusion.1), channel_id=1, source_target_pairs={{0,2},{2,0},{1,3},{3,1},{4,6},{6,4},{5,7},{7,5},{8,10},{10,8},{9,1... | collective-permute-start | bytes 3145736 | tf_op jit(solution)/shard_map/ppermute | solution.py:1064
  94.4 41.8 %collective-permute-start.9 = (bf16[2,2,128,1024]{3,2,1,0:T(8,128)(2,1)S(1)}, bf16[2,2,128,1024]{3,2,1,0:T(8,128)(2,1)}, u32[]{:S(2)}, u32[]{:S(2)}) collective-permute-start(bf16[2,2,128,1024]{3,2,1,0:T(8,128)(2,1)S(1)} %pad_maximum_fusion), channel_id=1, source_target_pairs={{0,1},{1,0},{2,3},{3,2},{4,5},{5,4},{6,7},{7,6},{8,9},{9,8},{10,11... | collective-permute-start | bytes 3145736 | tf_op jit(solution)/shard_map/ppermute | solution.py:1064
  97.9 40.5 %collective-permute-start.11 = (bf16[2,2,128,1024]{3,2,1,0:T(8,128)(2,1)S(1)}, bf16[2,2,128,1024]{3,2,1,0:T(8,128)(2,1)S(1)}, u32[]{:S(2)}, u32[]{:S(2)}) collective-permute-start(bf16[2,2,128,1024]{3,2,1,0:T(8,128)(2,1)S(1)} %pad_maximum_fusion.1), channel_id=1, source_target_pairs={{0,1},{1,0},{2,3},{3,2},{4,5},{5,4},{6,7},{7,6},{8,9},{9,8},{10,11... | collective-permute-start | bytes 3145736 | tf_op jit(solution)/shard_map/ppermute | solution.py:1064
  168.1 29.5 %all-to-all-start.1 = ((bf16[16,64,256]{2,1,0:T(8,128)(2,1)}), bf16[16,64,256]{2,1,0:T(8,128)(2,1)S(1)}, u32[]{:S(2)}, u32[]{:S(2)}) async-start(bf16[16,64,256]{2,1,0:T(8,128)(2,1)} %get-tuple-element.42), calls=%async_computation.1 | async-start | bytes 1048576 | tf_op jit(solution)/shard_map/all_to_all | solution.py:1226
  180.6 248.7 %reduce-scatter.2.cloned.1.call-start = ((), (), s32[]{:S(2)}) async-start(), calls=%async_computation.7 | async-start | bytes 10027008 | tf_op jit(solution)/shard_map/reduce_scatter | solution.py:1265
  180.8 37.3 %collective-permute-start = (bf16[2,128,1024]{2,1,0:T(8,128)(2,1)}, bf16[2,128,1024]{2,1,0:T(8,128)(2,1)}, u32[]{:S(2)}, u32[]{:S(2)}) collective-permute-start(bf16[2,128,1024]{2,1,0:T(8,128)(2,1)} %param.18), channel_id=1, source_target_pairs={{0,1},{1,0},{2,3},{3,2},{4,5},{5,4},{6,7},{7,6},{8,9},{9,8},{10,11... | collective-permute-start | bytes 1572872 | tf_op jit(solution)/shard_map/ppermute | solution.py:1064
  181.2 37.0 %collective-permute-start.1 = (bf16[2,128,1024]{2,1,0:T(8,128)(2,1)S(1)}, bf16[2,128,1024]{2,1,0:T(8,128)(2,1)S(1)}, u32[]{:S(2)}, u32[]{:S(2)}) collective-permute-start(bf16[2,128,1024]{2,1,0:T(8,128)(2,1)S(1)} %copy-done.7), channel_id=1, source_target_pairs={{0,1},{1,0},{2,3},{3,2},{4,5},{5,4},{6,7},{7,6},{8,9},{9,8},{10,11... | collective-permute-start | bytes 1572872 | tf_op jit(solution)/shard_map/ppermute | solution.py:1064
  204.6 13.6 %collective-permute-start.16 = (bf16[256,1024]{1,0:T(8,128)(2,1)S(1)}, bf16[256,1024]{1,0:T(8,128)(2,1)}, u32[]{:S(2)}, u32[]{:S(2)}) collective-permute-start(bf16[256,1024]{1,0:T(8,128)(2,1)S(1)} %get-tuple-element.96), channel_id=1, source_target_pairs={{0,1},{1,0},{2,3},{3,2},{4,5},{5,4},{6,7},{7,6},{8,9},{9,8},{10,11... | collective-permute-start | bytes 1572872 | tf_op jit(solution)/shard_map/ppermute | solution.py:1064
  205.5 12.7 %collective-permute-start.17 = (bf16[256,1024]{1,0:T(8,128)(2,1)S(1)}, bf16[256,1024]{1,0:T(8,128)(2,1)}, u32[]{:S(2)}, u32[]{:S(2)}) collective-permute-start(bf16[256,1024]{1,0:T(8,128)(2,1)S(1)} %get-tuple-element.95), channel_id=1, source_target_pairs={{0,1},{1,0},{2,3},{3,2},{4,5},{5,4},{6,7},{7,6},{8,9},{9,8},{10,11... | collective-permute-start | bytes 1572872 | tf_op jit(solution)/shard_map/ppermute | solution.py:1064
  259.7 27.4 %all-to-all-start.2 = ((bf16[16,72,256]{2,1,0:T(8,128)(2,1)}), bf16[16,72,256]{2,1,0:T(8,128)(2,1)S(1)}, u32[]{:S(2)}, u32[]{:S(2)}) async-start(bf16[16,72,256]{2,1,0:T(8,128)(2,1)} %get-tuple-element.56), calls=%async_computation.2 | async-start | bytes 1179648 | tf_op jit(solution)/shard_map/all_to_all | solution.py:1258
  267.7 116.7 %collective-permute-start.18 = (bf16[256,1024]{1,0:T(8,128)(2,1)}, bf16[256,1024]{1,0:T(8,128)(2,1)}, u32[]{:S(2)}, u32[]{:S(2)}) collective-permute-start(bf16[256,1024]{1,0:T(8,128)(2,1)} %get-tuple-element.48), channel_id=1, source_target_pairs={{0,1},{1,0},{2,3},{3,2},{4,5},{5,4},{6,7},{7,6},{8,9},{9,8},{10,11... | collective-permute-start | bytes 1572872 | tf_op jit(solution)/shard_map/ppermute | solution.py:1064
  319.0 58.1 %all-to-all-start.3 = ((bf16[16,192,256]{2,1,0:T(8,128)(2,1)}), bf16[16,192,256]{2,1,0:T(8,128)(2,1)S(1)}, u32[]{:S(2)}, u32[]{:S(2)}) async-start(bf16[16,192,256]{2,1,0:T(8,128)(2,1)} %get-tuple-element.62), calls=%async_computation.3 | async-start | bytes 3145728 | tf_op jit(solution)/shard_map/all_to_all | solution.py:1270
  377.1 26.6 %all-to-all-start.4 = ((bf16[16,72,192]{2,1,0:T(8,128)(2,1)}), bf16[16,72,192]{2,1,0:T(8,128)(2,1)S(1)}, u32[]{:S(2)}, u32[]{:S(2)}) async-start(bf16[16,72,192]{2,1,0:T(8,128)(2,1)} %pad_maximum_fusion.3), calls=%async_computation.4 | async-start | bytes 1179648 | tf_op jit(solution)/shard_map/all_to_all | solution.py:1298
  404.9 11.7 %collective-permute-start.22 = (f32[8,33,192]{2,0,1:T(8,128)}, f32[8,33,192]{2,0,1:T(8,128)}, u32[]{:S(2)}, u32[]{:S(2)}) collective-permute-start(f32[8,33,192]{2,0,1:T(8,128)} %pad_maximum_fusion.7), channel_id=1, source_target_pairs={{0,1},{1,0},{2,3},{3,2},{4,5},{5,4},{6,7},{7,6},{8,9},{9,8},{10,11... | collective-permute-start | bytes 608264 | tf_op jit(solution)/shard_map/ppermute | solution.py:1064
  (52 other events, 464.8 us)
Sparse Core Ops, SparseCore 0:
  13.3 154.3 all-gather.5
  169.8 63.3 all-gather.3
  259.8 164.5 reduce-scatter.1
